TPU v7x, 256 devices: a whole 4x4x8 slice. The times are simulated.
256 devices in a mesh: seq: 64 (over z, x, core), head: 4 (over y).
Axes of the slice: x: 4, y: 4, z: 8, core: 2. Of those that a mesh axis runs over, the one named last changes fastest.
Arguments:
- states: bfloat16 [32768, 2048], P('seq'), may hold values from -6 to 6
- inner_weight: bfloat16 [2048, 4096], P(None, 'head'), may hold values from -0.125 to 0.125
- gate_weight: bfloat16 [2048, 4096], P(None, 'head'), may hold values from -1 to 1
- state_weight: bfloat16 [2048, 256], replicated, may hold values from -0.125 to 0.125
- step_weight: bfloat16 [2048, 32], P(None, 'head'), may hold values from -0.125 to 0.125
- step_bias: float32 [32], P('head'), may hold values from -4 to -2
- decay_rate: float32 [32], P('head'), may hold values from 0 to 1
- skip_gain: float32 [32], P('head'), may hold values from 0.5 to 1.5
- conv_inner: float32 [4, 4096], P(None, 'head'), may hold values from -3 to 3
- conv_state: float32 [4, 256], replicated, may hold values from -3 to 3
- norm_gain: float32 [4096], P('head'), may hold values from 0.5 to 2
- value_weight: float32 [4096], P('head'), may hold values from -0.09375 to 0.09375
- rewards: float32 [32768], P('seq'), may hold values from -4 to 4
- done_flags: int32 [32768], P('seq'), may hold values from 0 to 1, as said below
- horizon: int32 [32768], P('seq'), may hold values from 1 to 8
Outputs:
- values: float32 [32768], P('seq')
- targets: float32 [32768], P('seq')
- value_loss: float32 [], replicated
Inputs may be any that keep to these rules, and one draw needn't show every extreme that they name: `done_flags`: exactly one time step of the trajectory has an episode end.
All inputs are finite; a program needn't handle non-finite values.
Results may differ from a plain program's by a relative error of at most 0.007.
Values may be sent and summed in bfloat16 or wider, within the bound.
A program may use at most 128 MiB of HBM per device.

v0:
```python
import math

import jax
import jax.numpy as jnp
from jax import lax
from jax.sharding import Mesh
from jax.sharding import PartitionSpec as P

D_INNER = 4096
KCONV = 4
NSTEP = 8
SEQ = ("seq_0", "seq_1", "seq_2")


DISCOUNT = 0.99
EXPECTILE = 0.7
EPSILON = 1e-05


def from_behind(block, axis, distance):
    devices = range(lax.axis_size(axis))
    route = [(i - distance, i) for i in devices if i - distance in devices]
    return lax.ppermute(block, axis, route)


def nothing_yet(array, identity):
    return jax.tree.map(
        lambda a, e: jnp.broadcast_to(jnp.asarray(e, a.dtype), a.shape), array, identity
    )


def entering(array, axes, combine, identity):
    before = start = nothing_yet(array, identity)
    running = array
    for axis in reversed(axes):
        size, mine = (lax.axis_size(axis), lax.axis_index(axis))
        pieces = jax.tree.map(lambda part: lax.all_gather(part, axis), running)
        inside, running = (start, start)
        for k in range(size):
            passed = k < mine
            running = combine(running, jax.tree.map(lambda part: part[k], pieces))
            inside = jax.tree.map(lambda new, old: jnp.where(passed, new, old), running, inside)
        before = combine(inside, before)
    return before


def from_everyone(array, axis):
    copies = jnp.broadcast_to(array, (lax.axis_size(axis), *array.shape))
    return lax.all_to_all(copies, axis, split_axis=0, concat_axis=0, tiled=True)


def taken_together(array, axis):
    everything = from_everyone(array, axis)
    return jnp.sum(everything, axis=0)


def causal_conv(rim_rows, projected, kernel):
    padded = jnp.concatenate([rim_rows.astype(jnp.float32), projected.astype(jnp.float32)], axis=0)
    length = projected.shape[0]
    summed = jnp.zeros(projected.shape, jnp.float32)
    for offset in range(kernel.shape[0]):
        summed = summed + kernel[offset] * padded[offset : offset + length]
    return jax.nn.silu(summed).astype(jnp.bfloat16)


def block_scan(inner, writes, readout, step_size, decay_rate, done_int, running_state):
    precise = lax.Precision.HIGHEST
    inputs = step_size[:, :, None] * inner.astype(jnp.float32)
    local_decay = jnp.cumsum(-decay_rate * step_size, axis=0)
    done_count = jnp.cumsum(done_int)
    done_before = done_count - done_int
    scores = jnp.dot(readout, writes.T, preferred_element_type=jnp.float32)
    positions = jnp.arange(inner.shape[0])
    causal_mask = (positions[:, None] >= positions[None, :]) & (
        done_before[:, None] == done_before[None, :]
    )
    decay_gap = local_decay[:, None, :] - local_decay[None, :, :]
    weights = scores[:, :, None] * jnp.exp(jnp.where(causal_mask[:, :, None], decay_gap, -jnp.inf))
    block_out = jnp.einsum("tsh,shp->thp", weights, inputs, precision=precise)
    carry_reach = jnp.exp(local_decay) * (done_before == 0)[:, None]
    readout_float = readout.astype(jnp.float32)
    block_out = block_out + carry_reach[:, :, None] * jnp.einsum(
        "tn,hpn->thp", readout_float, running_state, precision=precise
    )
    tail_weight = (
        jnp.exp(local_decay[-1][None, :] - local_decay)
        * (done_count[-1] - done_before == 0)[:, None]
    )
    block_state = jnp.einsum(
        "shp,sn->hpn",
        tail_weight[:, :, None] * inputs,
        writes.astype(jnp.float32),
        precision=precise,
    )
    block_decay = jnp.exp(local_decay[-1]) * (done_count[-1] == 0)
    return (block_out, block_decay[:, None, None] * running_state + block_state, block_decay)


def nstep_targets(reward_ext, alive_ext, value_ext, horizon, length):
    targets = jnp.zeros((length,), jnp.float32)
    survive = jnp.ones((length,), jnp.float32)
    for offset in range(NSTEP + 1):
        factor = DISCOUNT**offset * survive
        targets = targets + jnp.where(
            offset < horizon, factor * reward_ext[offset : offset + length], 0.0
        )
        targets = targets + jnp.where(
            offset == horizon, factor * value_ext[offset : offset + length], 0.0
        )
        survive = survive * alive_ext[offset : offset + length]
    return targets


def expectile_terms(targets, values):
    residual = targets - values
    return jnp.where(residual < 0, 1.0 - EXPECTILE, EXPECTILE) * residual * residual


def link_states(earlier, latter):
    return (earlier[0] * latter[0], latter[0][:, None, None] * earlier[1] + latter[1])


def per_device(
    states,
    inner_weight,
    gate_weight,
    state_weight,
    step_weight,
    step_bias,
    decay_rate,
    skip_gain,
    conv_inner,
    conv_state,
    norm_gain,
    value_weight,
    rewards,
    done_flags,
    horizon,
):
    token_count = states.shape[0]
    head_count = step_bias.shape[0]
    inner_width = inner_weight.shape[1]
    head_width = inner_width // head_count
    state_width = state_weight.shape[1] // 2
    inner_pre = jnp.dot(states, inner_weight, preferred_element_type=jnp.float32).astype(
        jnp.bfloat16
    )
    gate_pre = jnp.dot(states, gate_weight, preferred_element_type=jnp.float32).astype(jnp.bfloat16)
    state_pre = jnp.dot(states, state_weight, preferred_element_type=jnp.float32).astype(
        jnp.bfloat16
    )
    step_size = jax.nn.softplus(
        jnp.dot(states, step_weight, preferred_element_type=jnp.float32) + step_bias
    )
    conv_lag = KCONV - 1
    edge_rows = jnp.concatenate(
        [inner_pre[token_count - conv_lag :], state_pre[token_count - conv_lag :]], axis=1
    )
    rim_rows = from_behind(edge_rows, SEQ, 1)
    inner_conv = causal_conv(rim_rows[:, :inner_width], inner_pre, conv_inner)
    state_conv = causal_conv(rim_rows[:, inner_width:], state_pre, conv_state)
    inner_heads = inner_conv.reshape(token_count, head_count, head_width)
    writes = state_conv[:, :state_width]
    readout = state_conv[:, state_width:]
    block_size = math.gcd(token_count, 256)
    running_state = jnp.zeros((head_count, head_width, state_width), jnp.float32)
    device_decay = jnp.ones((head_count,), jnp.float32)
    outputs = []
    for block_index in range(token_count // block_size):
        first_row = block_index * block_size
        last_row = first_row + block_size
        block_out, running_state, block_decay = block_scan(
            inner_heads[first_row:last_row],
            writes[first_row:last_row],
            readout[first_row:last_row],
            step_size[first_row:last_row],
            decay_rate,
            done_flags[first_row:last_row],
            running_state,
        )
        device_decay = device_decay * block_decay
        outputs.append(block_out)
    mixed_heads = jnp.concatenate(outputs, axis=0)
    identity = (jnp.ones_like(device_decay), jnp.zeros_like(running_state))
    carried = entering((device_decay, running_state), SEQ, link_states, identity)[1]
    full_decay = jnp.cumsum(-decay_rate * step_size, axis=0)
    full_before = jnp.cumsum(done_flags) - done_flags
    carry_reach = jnp.exp(full_decay) * (full_before == 0)[:, None]
    correction = jnp.einsum(
        "tn,hpn->thp", readout.astype(jnp.float32), carried, precision=lax.Precision.HIGHEST
    )
    mixed_heads = mixed_heads + carry_reach[:, :, None] * correction
    mixed_heads = mixed_heads + skip_gain[None, :, None] * inner_heads.astype(jnp.float32)
    gated = mixed_heads.reshape(token_count, inner_width) * jax.nn.silu(
        gate_pre.astype(jnp.float32)
    )
    square_part = jnp.sum(gated * gated, axis=1)
    value_part = jnp.sum(gated * (norm_gain * value_weight), axis=1)
    square_sum, value_sum = lax.psum((square_part, value_part), "head")
    values = value_sum * lax.rsqrt(square_sum / D_INNER + EPSILON)
    alive = 1.0 - done_flags.astype(jnp.float32)
    leading = jnp.stack([rewards[:NSTEP], alive[:NSTEP], values[:NSTEP]], axis=0)
    following = from_behind(leading, SEQ, -1)
    targets = nstep_targets(
        jnp.concatenate([rewards, following[0]]),
        jnp.concatenate([alive, following[1]]),
        jnp.concatenate([values, following[2]]),
        horizon,
        token_count,
    )
    local_loss = jnp.sum(expectile_terms(targets, values))
    value_loss = taken_together(local_loss, SEQ) / (token_count * lax.axis_size(SEQ))
    return (values, targets, value_loss)


def solution(mesh):
    torus = Mesh(
        mesh.devices.reshape(8, 4, 2, mesh.shape["head"]), ("seq_0", "seq_1", "seq_2", "head")
    )
    placed = (
        P(SEQ, None),
        P(None, "head"),
        P(None, "head"),
        P(),
        P(None, "head"),
        P("head"),
        P("head"),
        P("head"),
        P(None, "head"),
        P(),
        P("head"),
        P("head"),
        P(SEQ),
        P(SEQ),
        P(SEQ),
    )
    return jax.shard_map(
        per_device, mesh=torus, in_specs=placed, out_specs=(P(SEQ), P(SEQ), P()), check_vma=False
    )
```

profile of v0, /device:TPU:1, one launch (start us, length us, event | category | flops | bytes accessed | tf_op | source)
XLA Modules:
  0.0 219.1 jit_solution(1889414927472992258)
XLA Ops:
  7.2 1.5 copy-done
  8.8 5.8 %fusion.186 = (f32[512,1024]{1,0:T(8,128)}, bf16[512,1024]{1,0:T(8,128)(2,1)S(1)}) fusion(bf16[512,2048]{1,0:T(8,128)(2,1)S(1)} %copy-done, bf16[2048,1024]{1,0:T(8,128)(2,1)} %param.16), kind=kOutput, calls=%fused_computation.285 | convolution fusion | flops 2148532224 | bytes 9437184 | tf_op jit(solution)/shard_map/dot_general | solution.py:145
  14.6 1.5 fusion.187
  16.2 4.5 %collective-permute-start = (bf16[3,1280]{1,0:T(4,128)(2,1)S(1)}, bf16[3,1280]{1,0:T(4,128)(2,1)S(1)}, u32[]{:S(2)}, u32[]{:S(2)}) collective-permute-start(bf16[3,1280]{1,0:T(4,128)(2,1)S(1)} %pad_maximum_fusion.2), channel_id=1, source_target_pairs={{0,4},{4,8},{8,12},{12,16},{16,20},{20,24},{24,28},{28,32},{32,36}... | collective-permute-start | bytes 23048 | tf_op jit(solution)/shard_map/ppermute | solution.py:23
  20.7 0.3 reduce-window.51
  21.2 0.1 slice_reduce_fusion.6
  21.3 0.6 slice.386
  21.9 0.3 reduce-window.45
  22.4 0.1 slice_reduce_fusion.7
  23.1 0.7 compare_convert_fusion
  23.9 0.7 compare_select_fusion.1
  24.6 0.6 reduce-window.55
  25.2 0.2 slice_reduce_fusion.1
  25.4 0.6 reduce-window.49
  26.0 0.2 slice_reduce_fusion.2
  26.2 0.6 slice.379
  27.4 0.6 compare_convert_fusion.1
  28.1 0.6 fusion.185
  28.9 0.7 multiply_reduce_fusion.2
  29.7 0.6 exponential_multiply_fusion.4
  30.3 4.4 %multiply_convert_fusion = bf16[512,1024]{1,0:T(8,128)(2,1)S(1)} fusion(f32[512,1024]{1,0:T(8,128)} %get-tuple-element.61, f32[3,1024]{1,0:T(4,128)S(1)} %slice_convert_fusion.2, f32[1024]{0:T(1024)S(1)} %bitcast.266, f32[1024]{0:T(1024)S(1)} %bitcast.267, f32[1024]{0:T(1024)S(1)} %bitcast.265, f32[1024]{0:T(1024)S(1)} %bitcast.264), kind=kLoop, calls=%fused_computation.31 | loop fusion | flops 7864320 | bytes 3174400 | tf_op jit(solution)/shard_map/convert_element_type | solution.py:63
  34.7 1.6 slice_convert_fusion
  36.3 2.6 %copy.65 = f32[256,1024]{0,1:T(8,128)} copy(f32[256,1024]{1,0:T(8,128)} %get-tuple-element.24) | data formatting | bytes 2097152 | tf_op jit(solution)/shard_map/convert_element_type | solution.py:68
  38.8 2.6 %copy.66 = f32[256,1024]{0,1:T(8,128)} copy(f32[256,1024]{1,0:T(8,128)} %get-tuple-element.23) | data formatting | bytes 2097152 | tf_op jit(solution)/shard_map/convert_element_type | solution.py:68
  41.4 2.1 multiply_convert_fusion.1
  43.5 1.9 convolution_add_fusion.1
  45.4 0.8 copy-done.1
  46.3 1.5 convolution_add_fusion
  47.8 1.8 all-gather.1
  49.6 8.0 %all-gather.2 = f32[4,1,8]{2,1,0:T(1,128)S(1)} all-gather(f32[1,1,8]{2,1,0:T(1,128)S(1)} %get-tuple-element.59), channel_id=1, replica_groups=mesh['seq_0'=8,'seq_1'=4,'seq_2'=2,'head'=4] {'seq_1'}, dimensions={0}, use_global_device_ids=true | all-gather | bytes 160 | tf_op jit(solution)/shard_map/all_gather | solution.py:37
  57.6 0.5 fusion.178
  58.1 7.1 %all-gather.12.cloned.1.call-done = f32[16,128,128]{2,1,0:T(8,128)} async-done(((f32[8,128,128]{2,1,0:T(8,128)}), f32[16,128,128]{2,1,0:T(8,128)}) %all-gather.12.cloned.1.call-update) | async-done | bytes 1048592 | tf_op jit(solution)/shard_map/all_gather | solution.py:37
  65.2 2.1 bitcast_add_fusion.4
  67.4 34.0 %all-gather.8.cloned.1.call-done = f32[4,8,128,128]{3,2,1,0:T(8,128)} async-done(((f32[1,8,128,128]{3,2,1,0:T(8,128)}), f32[4,8,128,128]{3,2,1,0:T(8,128)}) %all-gather.8.cloned.1.call-update) | async-done | bytes 2097168 | tf_op jit(solution)/shard_map/all_gather | solution.py:37
  101.4 2.6 %multiply_add_fusion = f32[1,8,128,128]{3,2,1,0:T(8,128)} fusion(f32[4,8,128,128]{3,2,1,0:T(8,128)} %all-gather.8.cloned.1.call-done, f32[8]{0:T(128)S(1)} %get-tuple-element.52, f32[8]{0:T(128)S(1)} %get-tuple-element.51, f32[8]{0:T(128)S(1)} %get-tuple-element.50, f32[8]{0:T(128)S(1)} %get-tuple-element.49), kind=kLoop, calls=%fused_computation.127 | loop fusion | flops 917504 | bytes 2621568 | tf_op jit(solution)/shard_map/add | solution.py:120
  104.1 1.1 reduce-window.59
  105.2 0.2 slice_reduce_fusion
  105.4 0.3 reduce-window.73
  105.9 0.6 mul.789
  106.5 12.9 %all-gather.3 = f32[8,1,8]{2,1,0:T(1,128)S(1)} all-gather(f32[1,1,8]{2,1,0:T(1,128)S(1)} %get-tuple-element.48), channel_id=1, replica_groups=mesh['seq_0'=8,'seq_1'=4,'seq_2'=2,'head'=4] {'seq_0'}, dimensions={0}, use_global_device_ids=true | all-gather | bytes 288 | tf_op jit(solution)/shard_map/all_gather | solution.py:37
  119.4 0.1 slice_reduce_fusion.5
  119.5 0.6 slice_bitcast_fusion.18
  120.1 0.6 slice_bitcast_fusion.23
  120.8 0.7 fusion.170
  121.4 0.7 fusion.138
  122.2 1.6 copy.67
  123.8 0.2 fusion.159
  124.0 0.2 fusion.164
  124.2 0.6 convolution_multiply_fusion.1
  124.8 0.1 copy-done.2
  124.8 0.6 convolution_multiply_fusion
  125.5 3.7 %fusion.32 = f32[256,8,128]{0,2,1:T(8,128)} fusion(f32[256,8,128]{0,2,1:T(8,128)S(1)} %convolution_multiply_fusion, f32[256,8]{0,1:T(8,128)S(1)} %get-tuple-element.22, f32[256,256]{1,0:T(8,128)S(1)} %fusion.159, pred[256,256]{1,0:T(8,128)(4,1)S(1)} %copy-done.9, f32[256,8,128]{0,2,1:T(8,128)S(1)} %bitcast.260, f32[256,8]{0,1:T(8,128)S(1)} %get-tuple-element.27), kind=kOutput, calls=%fused_computation.37 | convolution fusion | flops 807403520 | bytes 3489792 | tf_op jit(solution)/shard_map/tsh,shp->thp/dot_general | solution.py:79
  129.3 3.7 %fusion.26 = f32[256,8,128]{0,2,1:T(8,128)} fusion(f32[256,8,128]{0,2,1:T(8,128)S(1)} %convolution_multiply_fusion.1, f32[256,8]{0,1:T(8,128)S(1)} %get-tuple-element.17, f32[256,256]{1,0:T(8,128)S(1)} %fusion.164, pred[256,256]{1,0:T(8,128)(4,1)S(1)} %get-tuple-element.68, f32[256,8,128]{0,2,1:T(8,128)S(1)} %bitcast.258, f32[256,8]{0,1:T(8,128)S(1)} %get-tuple-element.28), kind=kOutput, calls=%fused_computation.35 | convolution fusion | flops 807403520 | bytes 3489792 | tf_op jit(solution)/shard_map/tsh,shp->thp/dot_general | solution.py:79
  133.0 26.1 %all-gather.10.cloned.1.call-done = f32[8,8,128,128]{3,2,1,0:T(8,128)} async-done(((f32[1,8,128,128]{3,2,1,0:T(8,128)}), f32[8,8,128,128]{3,2,1,0:T(8,128)}) %all-gather.10.cloned.1.call-update) | async-done | bytes 4194320 | tf_op jit(solution)/shard_map/all_gather | solution.py:37
  159.2 7.3 %fusion.12 = f32[512,8,128]{0,2,1:T(8,128)} fusion(f32[256,8,128]{0,2,1:T(8,128)} %fusion.32, f32[256,8,128]{0,2,1:T(8,128)} %fusion.26, f32[512,8,128]{0,2,1:T(8,128)} %bitcast.261, f32[8]{0:T(128)} %param.22, f32[512,8]{0,1:T(8,128)S(1)} %copy-done.13, f32[8,8,128,128]{3,2,1,0:T(8,128)} %all-gather.10.cloned.1.call-done, ...), kind=kOutput, calls=%fused_computation.18 | convolution fusion | flops 813563904 | bytes 13784302 | tf_op jit(solution)/shard_map/tn,hpn->thp/dot_general | solution.py:189
  166.5 2.9 %copy.68 = f32[512,1024]{1,0:T(8,128)} copy(f32[512,1024]{0,1:T(8,128)} %bitcast.262) | data formatting | bytes 4194304 | tf_op jit(solution)/shard_map/reshape | solution.py:194
  169.4 5.8 %multiply_reduce_fusion = (f32[512]{0:T(512)S(1)}, f32[512]{0:T(512)S(1)}) fusion(f32[1024]{0:T(1024)S(1)} %copy-done.22, f32[512,1024]{1,0:T(8,128)} %copy.68, bf16[512,2048]{1,0:T(8,128)(2,1)S(1)} %copy-done, bf16[2048,1024]{1,0:T(8,128)(2,1)} %param.17), kind=kOutput, calls=%fused_computation.19 | convolution fusion | flops 2153249792 | bytes 8396800 | tf_op jit(solution)/shard_map/dot_general | solution.py:148
  175.2 8.5 %all-reduce = (f32[512]{0:T(512)S(1)}, f32[512]{0:T(512)S(1)}) all-reduce(f32[512]{0:T(512)S(1)} %get-tuple-element.4, f32[512]{0:T(512)S(1)} %get-tuple-element.3), channel_id=1, replica_groups=mesh['seq_0'=8,'seq_1'=4,'seq_2'=2,'head'=4] {'head'}, use_global_device_ids=true, to_apply=%region_13.14 | all-reduce | flops 1024 | bytes 8192 | tf_op jit(solution)/shard_map/psum | solution.py:199
  183.8 4.6 %collective-permute-start.1 = (f32[3,8]{1,0:T(4,128)S(1)}, f32[3,8]{1,0:T(4,128)S(1)}, u32[]{:S(2)}, u32[]{:S(2)}) collective-permute-start(f32[3,8]{1,0:T(4,128)S(1)} %pad_maximum_fusion.6), channel_id=1, source_target_pairs={{4,0},{8,4},{12,8},{16,12},{20,16},{24,20},{28,24},{32,28},{36,32}... | collective-permute-start | bytes 296 | tf_op jit(solution)/shard_map/ppermute | solution.py:23
  188.4 2.3 %collective-permute-done.1 = f32[3,8]{1,0:T(4,128)S(1)} collective-permute-done((f32[3,8]{1,0:T(4,128)S(1)}, f32[3,8]{1,0:T(4,128)S(1)}, u32[]{:S(2)}, u32[]{:S(2)}) %collective-permute-start.1) | collective-permute-done | bytes 128 | tf_op jit(solution)/shard_map/ppermute | solution.py:23
  190.7 1.3 fusion.175
  192.0 0.7 broadcast_in_dim.94
  192.7 17.5 %all_to_all.6 = f32[64,1,1]{2,1,0:T(1,128)S(1)} all-to-all(f32[64,1,1]{2,1,0:T(1,128)S(1)} %broadcast_in_dim.94), channel_id=1, replica_groups=mesh['seq_0'=8,'seq_1'=4,'seq_2'=2,'head'=4] {'seq_0','seq_1','seq_2'}, dimensions={0} | all-to-all | bytes 512 | tf_op jit(solution)/shard_map/all_to_all | solution.py:49
  210.2 0.7 reduce_sum.39
  (142 shorter events, 1.5 us)
Async XLA Ops:
  7.2 1.6 copy-start
  7.2 7.5 %copy-start.7 = (bf16[2048,256]{1,0:T(8,128)(2,1)S(1)}, bf16[2048,256]{1,0:T(8,128)(2,1)}, u32[]{:S(2)}) copy-start(bf16[2048,256]{1,0:T(8,128)(2,1)} %param.18) | copy-start | bytes 3145732
  7.2 58.0 %all-gather.12.cloned.1.call-start = ((), (), s32[]{:S(2)}) async-start(), calls=%async_computation.3 | async-start | bytes 1572864 | tf_op jit(solution)/shard_map/all_gather | solution.py:37
  14.6 6.1 %copy-start.8 = (s32[512]{0:T(512)S(1)}, s32[512]{0:T(512)}, u32[]{:S(2)}) copy-start(s32[512]{0:T(512)} %param.28) | copy-start | bytes 6148
  14.6 9.2 %copy-start.49 = (f32[8]{0:T(128)S(1)}, f32[8]{0:T(128)}, u32[]{:S(2)}) copy-start(f32[8]{0:T(128)} %param.21) | copy-start | bytes 100
  14.6 9.3 %copy-start.10 = (bf16[2048,8]{0,1:T(8,128)(2,1)S(1)}, bf16[2048,8]{0,1:T(8,128)(2,1)}, u32[]{:S(2)}) copy-start(bf16[2048,8]{0,1:T(8,128)(2,1)} %param.19) | copy-start | bytes 98308
  14.6 9.3 %copy-start.43 = (f32[8]{0:T(128)S(1)}, f32[8]{0:T(128)}, u32[]{:S(2)}) copy-start(f32[8]{0:T(128)} %param.20) | copy-start | bytes 100
  16.2 11.9 %copy-start.23 = (f32[4,256]{1,0:T(4,128)S(1)}, f32[4,256]{1,0:T(4,128)}, u32[]{:S(2)}) copy-start(f32[4,256]{1,0:T(4,128)} %param.24) | copy-start | bytes 12292
  16.2 12.5 %copy-start.12 = (f32[4,1024]{1,0:T(4,128)S(1)}, f32[4,1024]{1,0:T(4,128)}, u32[]{:S(2)}) copy-start(f32[4,1024]{1,0:T(4,128)} %param.23) | copy-start | bytes 49156
  16.2 14.1 %collective-permute-start = (bf16[3,1280]{1,0:T(4,128)(2,1)S(1)}, bf16[3,1280]{1,0:T(4,128)(2,1)S(1)}, u32[]{:S(2)}, u32[]{:S(2)}) collective-permute-start(bf16[3,1280]{1,0:T(4,128)(2,1)S(1)} %pad_maximum_fusion.2), channel_id=1, source_target_pairs={{0,4},{4,8},{8,12},{12,16},{16,20},{20,24},{24,28},{28,32},{32,36}... | collective-permute-start | bytes 23048 | tf_op jit(solution)/shard_map/ppermute | solution.py:23
  23.9 3.5 %copy-start.24 = (f32[8]{0:T(128)}, f32[8]{0:T(128)S(1)}, u32[]{:S(2)}) copy-start(f32[8]{0:T(128)S(1)} %neg.26) | copy-start | bytes 100
  36.3 5.1 %copy-start.17 = (f32[1,256]{1,0:T(1,128)S(1)}, f32[1,256]{1,0:T(1,128)}, u32[]{:S(2)}) copy-start(f32[1,256]{1,0:T(1,128)} %get-tuple-element.42) | copy-start | bytes 3076
  36.3 5.1 %copy-start.18 = (f32[1,256]{1,0:T(1,128)S(1)}, f32[1,256]{1,0:T(1,128)}, u32[]{:S(2)}) copy-start(f32[1,256]{1,0:T(1,128)} %get-tuple-element.43) | copy-start | bytes 3076
  36.3 5.2 %copy-start.19 = (f32[1,256]{1,0:T(1,128)S(1)}, f32[1,256]{1,0:T(1,128)}, u32[]{:S(2)}) copy-start(f32[1,256]{1,0:T(1,128)} %get-tuple-element.44) | copy-start | bytes 3076
  36.3 7.2 %copy-start.33 = (f32[8]{0:T(128)S(1)}, f32[8]{0:T(128)}, u32[]{:S(2)}) copy-start(f32[8]{0:T(128)} %get-tuple-element.72) | copy-start | bytes 100
  38.8 7.4 %copy-start.32 = (f32[8]{0:T(128)S(1)}, f32[8]{0:T(128)}, u32[]{:S(2)}) copy-start(f32[8]{0:T(128)} %get-tuple-element.71) | copy-start | bytes 100
  41.4 4.8 %copy-start.4 = (f32[256,1024]{0,1:T(8,128)S(1)}, f32[256,1024]{0,1:T(8,128)}, u32[]{:S(2)}) copy-start(f32[256,1024]{0,1:T(8,128)} %copy.66) | copy-start | bytes 3145732
  43.5 4.3 %copy-start.48 = (f32[8]{0:T(128)S(1)}, f32[8]{0:T(128)}, u32[]{:S(2)}) copy-start(f32[8]{0:T(128)} %get-tuple-element.5) | copy-start | bytes 100
  45.4 0.8 copy-start.1
  47.8 53.7 %all-gather.8.cloned.1.call-start = ((), (), s32[]{:S(2)}) async-start(), calls=%async_computation.1 | async-start | bytes 2621440 | tf_op jit(solution)/shard_map/all_gather | solution.py:37
  49.6 15.6 %copy-start.30 = (f32[8]{0:T(128)}, f32[8]{0:T(128)S(1)}, u32[]{:S(2)}) copy-start(f32[8]{0:T(128)S(1)} %get-tuple-element.60) | copy-start | bytes 100
  58.1 45.9 %copy-start.26 = (f32[8]{0:T(128)}, f32[8]{0:T(128)S(1)}, u32[]{:S(2)}) copy-start(f32[8]{0:T(128)S(1)} %get-tuple-element.52) | copy-start | bytes 100
  58.1 45.9 %copy-start.28 = (f32[8]{0:T(128)}, f32[8]{0:T(128)S(1)}, u32[]{:S(2)}) copy-start(f32[8]{0:T(128)S(1)} %get-tuple-element.58) | copy-start | bytes 100
  67.3 36.7 %copy-start.25 = (f32[8]{0:T(128)S(1)}, f32[8]{0:T(128)}, u32[]{:S(2)}) copy-start(f32[8]{0:T(128)} %copy-done.24) | copy-start | bytes 100
  67.3 38.6 %copy-start.20 = (f32[1024]{0:T(1024)S(1)}, f32[1024]{0:T(1024)}, u32[]{:S(2)}) copy-start(f32[1024]{0:T(1024)} %param.25) | copy-start | bytes 12292
  67.3 38.6 %copy-start.21 = (f32[1024]{0:T(1024)S(1)}, f32[1024]{0:T(1024)}, u32[]{:S(2)}) copy-start(f32[1024]{0:T(1024)} %param.26) | copy-start | bytes 12292
  67.3 52.8 %copy-start.14 = (f32[512]{0:T(512)S(1)}, f32[512]{0:T(512)}, u32[]{:S(2)}) copy-start(f32[512]{0:T(512)} %param.27) | copy-start | bytes 6148
  67.3 91.7 %all-gather.10.cloned.1.call-start = ((), (), s32[]{:S(2)}) async-start(), calls=%async_computation.2 | async-start | bytes 4718592 | tf_op jit(solution)/shard_map/all_gather | solution.py:37
  67.4 36.6 %copy-start.34 = (f32[8]{0:T(128)}, f32[8]{0:T(128)S(1)}, u32[]{:S(2)}) copy-start(f32[8]{0:T(128)S(1)} %get-tuple-element.49) | copy-start | bytes 100
  67.4 53.3 %copy-start.36 = (f32[8]{0:T(128)}, f32[8]{0:T(128)S(1)}, u32[]{:S(2)}) copy-start(f32[8]{0:T(128)S(1)} %get-tuple-element.50) | copy-start | bytes 100
  67.4 53.3 %copy-start.38 = (f32[8]{0:T(128)}, f32[8]{0:T(128)S(1)}, u32[]{:S(2)}) copy-start(f32[8]{0:T(128)S(1)} %get-tuple-element.51) | copy-start | bytes 100
  119.5 1.3 copy-start.15
  123.8 1.1 copy-start.2
  123.8 1.7 copy-start.5
  123.8 1.7 copy-start.9
  125.4 3.8 %copy-start.3 = (f32[256,1024]{0,1:T(8,128)S(1)}, f32[256,1024]{0,1:T(8,128)}, u32[]{:S(2)}) copy-start(f32[256,1024]{0,1:T(8,128)} %copy.65) | copy-start | bytes 3145732
  129.2 29.9 %copy-start.6 = (f32[16,128,128]{2,1,0:T(8,128)S(1)}, f32[16,128,128]{2,1,0:T(8,128)}, u32[]{:S(2)}) copy-start(f32[16,128,128]{2,1,0:T(8,128)} %all-gather.12.cloned.1.call-done) | copy-start | bytes 3145732
  129.2 29.9 %copy-start.13 = (f32[512,8]{0,1:T(8,128)S(1)}, f32[512,8]{0,1:T(8,128)}, u32[]{:S(2)}) copy-start(f32[512,8]{0,1:T(8,128)} %fusion.170) | copy-start | bytes 49156
  129.2 29.9 %copy-start.27 = (f32[8]{0:T(128)S(1)}, f32[8]{0:T(128)}, u32[]{:S(2)}) copy-start(f32[8]{0:T(128)} %copy-done.26) | copy-start | bytes 100
  129.2 29.9 %copy-start.29 = (f32[8]{0:T(128)S(1)}, f32[8]{0:T(128)}, u32[]{:S(2)}) copy-start(f32[8]{0:T(128)} %copy-done.28) | copy-start | bytes 100
  129.2 29.9 %copy-start.31 = (f32[8]{0:T(128)S(1)}, f32[8]{0:T(128)}, u32[]{:S(2)}) copy-start(f32[8]{0:T(128)} %copy-done.30) | copy-start | bytes 100
  129.2 29.9 %copy-start.35 = (f32[8]{0:T(128)S(1)}, f32[8]{0:T(128)}, u32[]{:S(2)}) copy-start(f32[8]{0:T(128)} %copy-done.34) | copy-start | bytes 100
  129.2 29.9 %copy-start.37 = (f32[8]{0:T(128)S(1)}, f32[8]{0:T(128)}, u32[]{:S(2)}) copy-start(f32[8]{0:T(128)} %copy-done.36) | copy-start | bytes 100
  129.2 29.9 %copy-start.39 = (f32[8]{0:T(128)S(1)}, f32[8]{0:T(128)}, u32[]{:S(2)}) copy-start(f32[8]{0:T(128)} %copy-done.38) | copy-start | bytes 100
  129.2 29.9 %copy-start.44 = (f32[8]{0:T(128)S(1)}, f32[8]{0:T(128)}, u32[]{:S(2)}) copy-start(f32[8]{0:T(128)} %get-tuple-element.12) | copy-start | bytes 100
  129.2 29.9 %copy-start.45 = (f32[8]{0:T(128)S(1)}, f32[8]{0:T(128)}, u32[]{:S(2)}) copy-start(f32[8]{0:T(128)} %get-tuple-element.13) | copy-start | bytes 100
  129.3 29.9 %copy-start.46 = (f32[8]{0:T(128)S(1)}, f32[8]{0:T(128)}, u32[]{:S(2)}) copy-start(f32[8]{0:T(128)} %get-tuple-element.33) | copy-start | bytes 100
  129.3 29.9 %copy-start.47 = (f32[8]{0:T(128)S(1)}, f32[8]{0:T(128)}, u32[]{:S(2)}) copy-start(f32[8]{0:T(128)} %get-tuple-element.34) | copy-start | bytes 100
  166.5 3.0 %copy-start.22 = (f32[1024]{0:T(1024)S(1)}, f32[1024]{0:T(1024)}, u32[]{:S(2)}) copy-start(f32[1024]{0:T(1024)} %mul.789) | copy-start | bytes 12292
  169.4 14.3 %copy-start.41 = (f32[1,8]{1,0:T(1,128)S(1)}, f32[1,8]{1,0:T(1,128)}, u32[]{:S(2)}) copy-start(f32[1,8]{1,0:T(1,128)} %get-tuple-element.73) | copy-start | bytes 100
  169.4 14.3 %copy-start.42 = (f32[1,8]{1,0:T(1,128)S(1)}, f32[1,8]{1,0:T(1,128)}, u32[]{:S(2)}) copy-start(f32[1,8]{1,0:T(1,128)} %get-tuple-element.74) | copy-start | bytes 100
  169.4 21.3 %copy-start.16 = (f32[512]{0:T(512)S(1)}, f32[512]{0:T(512)}, u32[]{:S(2)}) copy-start(f32[512]{0:T(512)} %copy-done.15) | copy-start | bytes 6148
  169.4 21.3 %copy-start.40 = (s32[512]{0:T(512)S(1)}, s32[512]{0:T(512)}, u32[]{:S(2)}) copy-start(s32[512]{0:T(512)} %param.29) | copy-start | bytes 6148
  183.7 27.8 %copy-start.11 = (f32[512]{0:T(512)}, f32[512]{0:T(512)S(1)}, u32[]{:S(2)}) copy-start(f32[512]{0:T(512)S(1)} %rsqrt_multiply_fusion) | copy-start | bytes 6148
  183.8 6.9 %collective-permute-start.1 = (f32[3,8]{1,0:T(4,128)S(1)}, f32[3,8]{1,0:T(4,128)S(1)}, u32[]{:S(2)}, u32[]{:S(2)}) collective-permute-start(f32[3,8]{1,0:T(4,128)S(1)} %pad_maximum_fusion.6), channel_id=1, source_target_pairs={{4,0},{8,4},{12,8},{16,12},{20,16},{24,20},{28,24},{32,28},{36,32}... | collective-permute-start | bytes 296 | tf_op jit(solution)/shard_map/ppermute | solution.py:23
Sparse Core Ops, SparseCore 0:
  47.9 17.2 all-gather.11
  67.5 33.9 all-gather.7
  104.1 54.8 all-gather.9
where the time goes:
time: 220 us; the launch traced here: 219 us
  waiting for transfers between devices  69.5 us (32%)
  blocking collectives  48.6 us (22%)
  matrix products  33.4 us (15%)
  other arithmetic  24.5 us (11%)
  between operations  17.5 us (8%)
  local copies, waits for them, and re-layouts  16.4 us (7%)
  starting transfers between devices  9.22 us (4%)
    all_gather x3, waiting for transfers between devices, entering(): pieces = jax.tree.map(lambda part: lax.all_gather(part, axis), running)  67.2 us
    all_gather x3, blocking collectives, entering(): pieces = jax.tree.map(lambda part: lax.all_gather(part, axis), running)  22.6 us
    all_to_all x1, blocking collectives, from_everyone(): return lax.all_to_all(copies, axis, split_axis=0, concat_axis=0, tiled=True)  17.5 us
    ppermute x2, starting transfers between devices, from_behind(): return lax.ppermute(block, axis, route)  9.1 us
    psum x1, blocking collectives, per_device(): square_sum, value_sum = lax.psum((square_part, value_part), 'head')  8.47 us
    dot_general x2, matrix products, block_scan(): block_out = jnp.einsum('tsh,shp->thp', weights, inputs, precision=precise)  7.38 us
    dot_general x1, matrix products, per_device(): jnp.einsum('tn,hpn->thp', readout.astype(jnp.float32), carried, precision...  7.31 us
    convert_element_type x2, other arithmetic, causal_conv(): return jax.nn.silu(summed).astype(jnp.bfloat16)  6.52 us
  transfers between devices with their start and end apart: 5, of which 4 were waited for; matrix products, arithmetic and copies ran while one was open for 11% of the time, Pallas kernels for 0%

commit v1 on v0

v1 whole, which is shorter than its diff:
```python
import functools

import jax
import jax.numpy as jnp
from jax import lax
from jax.experimental import pallas as pl
from jax.experimental.pallas import tpu as pltpu
from jax.sharding import Mesh
from jax.sharding import PartitionSpec as P

SEQ = ("seq_0", "seq_1", "seq_2")
MESH = pl.DeviceIdType.MESH
F32 = jnp.float32
BF16 = jnp.bfloat16

KCONV = 4
NSTEP = 8
DISCOUNT = 0.99
EXPECTILE = 0.7
EPSILON = 1e-05

HALO = 16
ROWS = 512
DEPTH = 2048
HEADS = 8
LANES = 128
WIDE = 256
TILES = HEADS * LANES // WIDE
PLANE = 8
DEPTHS = 8
PEERS = 4


def silu(value):
    half = 0.5 * value
    return half + half * jnp.tanh(half)


def dot(a, b):
    return jnp.dot(a, b, preferred_element_type=F32)


def three_pieces(value):
    high = value.astype(BF16).astype(F32)
    rest = value - high
    middle = rest.astype(BF16).astype(F32)
    return high, middle, rest - middle


def decay_rows(row):
    high, middle, low = three_pieces(row)
    place = lax.broadcasted_iota(jnp.int32, (16, LANES), 0)
    rows = jnp.where(place == 0, high, 0.0)
    rows = jnp.where(place == 1, middle, rows)
    return jnp.where(place == 2, low, rows).astype(BF16)


def down(row, rows=LANES):
    return jnp.broadcast_to(row, (rows, row.shape[1])).T


def kernel(
    seq_total,
    states,
    w_in,
    w_gate,
    w_state,
    w_step,
    bias,
    rate,
    skip,
    taps_in,
    taps_st,
    gain,
    weight,
    rewards,
    done,
    horizon,
    values_out,
    targets_out,
    loss_out,
    xs,
    wi,
    wg,
    ws,
    wt_in,
    wt,
    tin,
    tst,
    gn,
    vw,
    rw,
    dn,
    hz,
    pre,
    xh,
    rdm,
    wtf,
    sc,
    lrow,
    dtrow,
    tail,
    decb,
    y,
    gs,
    rs,
    send1,
    recv1,
    inside,
    reach_in,
    send2,
    recv2,
    send3,
    recv3,
    send4,
    recv4,
    part,
    recvh,
    recvn,
    ext,
    recvr,
    coef,
    loss1,
    recvl1,
    loss2,
    recvl2,
    local_sem,
    tile_sem,
    halo_sem,
    s1,
    r1,
    s2,
    r2,
    s3,
    r3,
    s4,
    r4,
    sh,
    rh,
    sn,
    rn,
    sl1,
    rl1,
    sl2,
    rl2,
):
    z, x, c, head = (lax.axis_index(name) for name in SEQ + ("head",))
    here = x * 2 + c
    place = z * PLANE + here
    total = DEPTHS * PLANE
    after = lax.rem(place + 1, total)
    before = lax.rem(place + total - 1, total)

    def of_place(at, at_head):
        return (lax.div(at, PLANE), lax.div(lax.rem(at, PLANE), 2), lax.rem(at, 2), at_head)

    def in_plane(q):
        return (z, lax.div(q, 2), lax.rem(q, 2), head)

    def in_depth(k):
        return (k, x, c, head)

    def in_head(k):
        return (z, x, c, k)

    def put(src, dst, ssem, rsem, device):
        return pltpu.make_async_remote_copy(
            src_ref=src, dst_ref=dst, send_sem=ssem, recv_sem=rsem, device_id=device, device_id_type=MESH
        )

    def others(me, count, act):
        def one(i, carry):
            act(lax.rem(me + i, count))
            return carry

        lax.fori_loop(1, count, one, 0)

    small = [
        (states, xs.at[pl.ds(HALO, ROWS), :]),
        (w_step, wt_in),
        (w_state, ws),
        (taps_st, tst),
        (taps_in, tin),
        (done, dn),
        (rewards, rw),
        (gain, gn),
        (weight, vw),
        (horizon, hz),
    ]
    local = [pltpu.make_async_copy(src, dst, local_sem.at[i]) for i, (src, dst) in enumerate(small)]

    def tile_copy(src, dst, slot, which):
        columns = pl.ds(pl.multiple_of(which * WIDE, WIDE), WIDE)
        return pltpu.make_async_copy(src.at[:, columns], dst.at[which], tile_sem.at[slot, which])

    def turned(j):
        return lax.rem(j + x, TILES)

    for copy in local[:3]:
        copy.start()
    for copy in local[3:]:
        copy.start()
    for j in range(TILES):
        tile_copy(w_in, wi, 0, turned(j)).start()
    for j in range(TILES):
        tile_copy(w_gate, wg, 1, j).start()

    barrier = pltpu.get_barrier_semaphore()

    def greet(device):
        pl.semaphore_signal(barrier, inc=1, device_id=device, device_id_type=MESH)

    others(here, PLANE, lambda q: greet(in_plane(q)))
    others(z, DEPTHS, lambda k: greet(in_depth(k)))
    others(head, PEERS, lambda k: greet(in_head(k)))
    greet(of_place(before, head))
    for k in range(PEERS):
        greet(of_place(after, k))
    pl.semaphore_wait(barrier, (PLANE - 1) + (DEPTHS - 1) + (PEERS - 1) + 1 + PEERS)

    halo = put(
        states.at[pl.ds(ROWS - HALO, HALO), :],
        xs.at[pl.ds(0, HALO), :],
        halo_sem.at[0],
        halo_sem.at[1],
        of_place(after, head),
    )
    halo.start()

    local[5].wait()
    local[6].wait()
    alive = 1.0 - dn[...].astype(F32)
    ext[...] = jnp.zeros((8, ROWS + LANES), F32)
    ext[0:1, 0:ROWS] = rw[...]
    ext[1:2, 0:ROWS] = alive
    rim = put(
        ext.at[:, pl.ds(0, LANES)], recvr, halo_sem.at[2], halo_sem.at[3], of_place(before, head)
    )
    rim.start()
    part[...] = jnp.zeros((8, ROWS), F32)

    local[0].wait()
    local[1].wait()
    wt[...] = jnp.concatenate(
        [wt_in[...].astype(F32), jnp.zeros((LANES - HEADS, DEPTH), F32)], axis=0
    ).astype(BF16)
    step_pre = lax.dot_general(
        xs[HALO : HALO + ROWS, :],
        wt[...],
        (((1,), (1,)), ((), ())),
        preferred_element_type=F32,
    ).T[0:HEADS, :]
    order = lax.broadcasted_iota(jnp.int32, (HEADS, ROWS), 0)
    bias_rows = jnp.zeros((HEADS, ROWS), F32)
    rate_rows = jnp.zeros((HEADS, ROWS), F32)
    for h in range(HEADS):
        bias_rows = jnp.where(order == h, bias[h], bias_rows)
        rate_rows = jnp.where(order == h, rate[h], rate_rows)
    step_pre = step_pre + bias_rows
    step = jnp.maximum(step_pre, 0.0) + jnp.log1p(jnp.exp(-jnp.abs(step_pre)))
    dtrow[...] = step
    done_rows = jnp.broadcast_to(dn[...].astype(F32), (HEADS, ROWS))
    blocks = ROWS // LANES
    pieces = three_pieces(-(rate_rows * step)) + (done_rows,)
    stacked = jnp.concatenate(
        [p[:, b * LANES : (b + 1) * LANES] for p in pieces for b in range(blocks)], axis=0
    ).astype(BF16)
    triangle = (
        lax.broadcasted_iota(jnp.int32, (LANES, LANES), 0)
        <= lax.broadcasted_iota(jnp.int32, (LANES, LANES), 1)
    ).astype(F32).astype(BF16)
    sums = dot(stacked, triangle)
    span = HEADS * blocks
    decays = sums[0:span] + sums[span : 2 * span] + sums[2 * span : 3 * span]
    dones = sums[3 * span : 4 * span]

    def joined(parts):
        found, offset = [], jnp.zeros((HEADS, 1), F32)
        for b in range(blocks):
            block = parts[b * HEADS : (b + 1) * HEADS, :] + offset
            offset = block[:, LANES - 1 : LANES]
            found.append(block)
        return jnp.concatenate(found, axis=1), offset

    running, last = joined(decays)
    done_to, done_all = joined(dones)
    done_before = done_to - done_rows
    lrow[...] = running
    tail[...] = jnp.where(done_before == done_all, jnp.exp(last - running) * step, 0.0)
    decb[...] = jnp.broadcast_to(jnp.where(done_all == 0.0, jnp.exp(last), 0.0), (HEADS, LANES))
    done_row = done_before[0:1, :]
    done_down = down(done_row)

    local[2].wait()
    local[3].wait()
    halo.wait_recv()
    inner_edge = jnp.where(place > 0, 1.0, 0.0)

    def convolved(taps):
        whole = pre[HALO : HALO + ROWS, :] * taps[KCONV - 1 : KCONV, :]
        for k in range(KCONV - 1):
            lag = KCONV - 1 - k
            whole = whole + pre[HALO - lag : HALO - lag + ROWS, :] * taps[k : k + 1, :]
        return silu(whole)

    pre[...] = dot(xs[...], ws[...])
    pre[0:HALO, :] = pre[0:HALO, :] * inner_edge
    state_conv = convolved(tst[...])
    wtf[...] = state_conv[:, 0:LANES].T
    writes_t = wtf[...].astype(BF16)
    readout = state_conv[:, LANES:WIDE]
    rdm[...] = jnp.where(done_down == 0.0, readout, 0.0)
    readout = readout.astype(BF16)
    for b in range(2):
        rows = slice(b * WIDE, (b + 1) * WIDE)
        upto = (b + 1) * WIDE
        scores = dot(readout[rows, :], writes_t[:, 0:upto])
        at_row = lax.broadcasted_iota(jnp.int32, (WIDE, LANES), 0) + b * WIDE
        for k in range(upto // LANES):
            columns = slice(k * LANES, (k + 1) * LANES)
            at_column = lax.broadcasted_iota(jnp.int32, (WIDE, LANES), 1) + k * LANES
            seen = (at_row >= at_column) & (done_down[rows, :] == done_row[:, columns])
            sc[rows, columns] = jnp.where(seen, scores[:, columns], 0.0)

    local[4].wait()

    def inner_tile(j, carry):
        which = turned(j)
        tile_copy(w_in, wi, 0, which).wait()
        pre[...] = dot(xs[...], wi[which])
        pre[0:HALO, :] = pre[0:HALO, :] * inner_edge
        taps = tin[:, pl.ds(pl.multiple_of(which * WIDE, WIDE), WIDE)]
        conv = convolved(taps).astype(BF16)
        for k in range(2):
            h = which * 2 + k
            inner = conv[:, k * LANES : (k + 1) * LANES]
            xh[h] = inner
            gained = dot((wtf[...] * tail[pl.ds(h, 1), :]).astype(BF16), inner).astype(BF16)
            lost = decay_rows(decb[pl.ds(h, 1), :])

            @pl.when(h == here)
            def _():
                recv1[h, 0:LANES, :] = gained
                recv1[h, LANES : LANES + 16, :] = lost

            @pl.when(h != here)
            def _():
                send1[h, 0:LANES, :] = gained
                send1[h, LANES : LANES + 16, :] = lost
                put(send1.at[h], recv1.at[here], s1.at[h], r1.at[here], in_plane(h)).start()

        return carry

    lax.fori_loop(0, TILES, inner_tile, 0)

    def gate_tile(j, carry):
        tile_copy(w_gate, wg, 1, j).wait()
        gate = silu(dot(xs[HALO : HALO + ROWS, :], wg[j]))
        for k in range(2):
            gs[j * 2 + k] = gate[:, k * LANES : (k + 1) * LANES]
        return carry

    lax.fori_loop(0, TILES // 2, gate_tile, 0)

    others(here, PLANE, lambda q: put(send1.at[q], recv1.at[q], s1.at[q], r1.at[q], in_plane(q)).wait_recv())

    def plane_step(q, carry):
        state, lasting = carry
        inside[q] = state
        reach_in[q] = jnp.broadcast_to(lasting, (8, LANES))
        lost = jnp.sum(recv1[q, LANES : LANES + 16, :].astype(F32), axis=0, keepdims=True)
        return lost * state + recv1[q, 0:LANES, :].astype(F32), lasting * lost

    state, lasting = lax.fori_loop(
        0, PLANE, plane_step, (jnp.zeros((LANES, LANES), F32), jnp.ones((1, LANES), F32))
    )
    send2[:, 0:16, :] = state.astype(BF16).reshape(DEPTHS, 16, LANES)
    send2[:, 16:32, :] = jnp.broadcast_to(decay_rows(lasting)[None], (DEPTHS, 16, LANES))
    recv2[z] = send2[z]
    others(z, DEPTHS, lambda k: put(send2.at[k], recv2.at[z], s2.at[k], r2.at[z], in_depth(k)).start())

    lax.fori_loop(TILES // 2, TILES, gate_tile, 0)

    others(z, DEPTHS, lambda k: put(send2.at[k], recv2.at[k], s2.at[k], r2.at[k], in_depth(k)).wait_recv())

    def depth_step(k, state):
        send3[k] = state.astype(BF16)
        lost = jnp.sum(recv2[k, 16:32, :].astype(F32), axis=0, keepdims=True)
        return lost * state + recv2[k, 0:16, :].astype(F32)

    lax.fori_loop(0, DEPTHS, depth_step, jnp.zeros((16, LANES), F32))
    recv3[z] = send3[z]
    others(z, DEPTHS, lambda k: put(send3.at[k], recv3.at[z], s3.at[k], r3.at[z], in_depth(k)).start())

    def own_scan(h, carry):
        across = lrow[pl.ds(h, 1), :]
        step_across = dtrow[pl.ds(h, 1), :]
        along = down(across)
        inner = xh[h]
        for b in range(2):
            rows = slice(b * WIDE, (b + 1) * WIDE)
            upto = (b + 1) * WIDE
            weights = []
            for k in range(upto // LANES):
                columns = slice(k * LANES, (k + 1) * LANES)
                gap = jnp.minimum(along[rows, :] - across[:, columns], 0.0)
                weights.append((jnp.exp(gap) * step_across[:, columns] * sc[rows, columns]).astype(BF16))
            mixed = dot(jnp.concatenate(weights, axis=1), inner[0:upto, :])
            y[h, rows, :] = mixed + skip[h] * inner[rows, :].astype(F32)
        rs[h] = (rdm[...] * jnp.exp(along)).astype(BF16)
        return carry

    lax.fori_loop(0, HEADS // 2, own_scan, 0)

    others(z, DEPTHS, lambda k: put(send3.at[k], recv3.at[k], s3.at[k], r3.at[k], in_depth(k)).wait_recv())
    entering = recv3[...].astype(F32).reshape(LANES, LANES)

    def hand_out(i, carry):
        q = lax.rem(here + i, PLANE)
        carried = (reach_in[q][0:1, :] * entering + inside[q]).astype(BF16)

        @pl.when(q == here)
        def _():
            recv4[q] = carried

        @pl.when(q != here)
        def _():
            send4[q] = carried
            put(send4.at[q], recv4.at[here], s4.at[q], r4.at[here], in_plane(q)).start()

        return carry

    lax.fori_loop(0, PLANE, hand_out, 0)

    lax.fori_loop(HEADS // 2, HEADS, own_scan, 0)

    local[7].wait()
    local[8].wait()
    local[9].wait()
    rim.wait_recv()
    is_last = place == total - 1
    ext[:, ROWS : ROWS + LANES] = jnp.where(is_last, 0.0, recvr[...])
    length = ROWS + LANES
    survive = jnp.ones((1, ROWS), F32)
    rewarded = jnp.zeros((1, ROWS), F32)
    for k in range(NSTEP + 1):
        ahead = ext[...] if k == 0 else pltpu.roll(ext[...], length - k, 1)
        factor = DISCOUNT**k * survive
        rewarded = rewarded + jnp.where(k < hz[...], factor * ahead[0:1, 0:ROWS], 0.0)
        coef[k : k + 1, :] = jnp.where(k == hz[...], factor, 0.0)
        survive = survive * ahead[1:2, 0:ROWS]
    coef[NSTEP + 1 : NSTEP + 2, :] = rewarded
    gn[...] = gn[...] * vw[...]

    others(here, PLANE, lambda q: put(send4.at[q], recv4.at[q], s4.at[q], r4.at[q], in_plane(q)).wait_recv())

    def mix(b, carry):
        rows = pl.ds(pl.multiple_of(b * LANES, LANES), LANES)
        squares = jnp.zeros((LANES, LANES), F32)
        valued = jnp.zeros((LANES, LANES), F32)
        for h in range(HEADS):
            mixed = y[h, rows, :] + dot(rs[h, rows, :], recv4[h])
            gated = mixed * gs[h, rows, :]
            squares = squares + gated * gated
            valued = valued + gated * gn[:, h * LANES : (h + 1) * LANES]
        part[0:1, rows] = jnp.sum(squares.T, axis=0, keepdims=True)
        part[1:2, rows] = jnp.sum(valued.T, axis=0, keepdims=True)
        return carry

    lax.fori_loop(0, ROWS // LANES, mix, 0)

    def to_peer(k):
        return put(part, recvh.at[head], sh.at[k], rh.at[head], in_head(k))

    def to_before(k):
        return put(
            part.at[:, pl.ds(0, LANES)], recvn.at[head], sn.at[k], rn.at[head], of_place(before, k)
        )

    others(head, PEERS, lambda k: to_peer(k).start())
    for k in range(PEERS):
        to_before(k).start()
    recvh[head] = part[...]
    others(head, PEERS, lambda k: put(part, recvh.at[k], sh.at[k], rh.at[k], in_head(k)).wait_recv())
    for k in range(PEERS):
        put(part.at[:, pl.ds(0, LANES)], recvn.at[k], sn.at[k], rn.at[k], of_place(after, k)).wait_recv()

    def normed(sums):
        return sums[1:2, :] * lax.rsqrt(sums[0:1, :] / (PEERS * HEADS * LANES) + EPSILON)

    own = normed(recvh[0] + recvh[1] + recvh[2] + recvh[3])
    following = normed(recvn[0] + recvn[1] + recvn[2] + recvn[3])
    following = jnp.where(is_last, 0.0, following)
    valued = jnp.broadcast_to(jnp.concatenate([own, following], axis=1), (8, length))
    targets = coef[NSTEP + 1 : NSTEP + 2, :]
    for k in range(NSTEP + 1):
        ahead = valued if k == 0 else pltpu.roll(valued, length - k, 1)
        targets = targets + coef[k : k + 1, :] * ahead[0:1, 0:ROWS]
    values_out[...] = own
    targets_out[...] = targets
    residual = targets - own
    terms = jnp.where(residual < 0, 1.0 - EXPECTILE, EXPECTILE) * residual * residual
    loss1[...] = jnp.broadcast_to(jnp.sum(terms, axis=1, keepdims=True), (8, LANES))
    others(here, PLANE, lambda q: put(loss1, recvl1.at[here], sl1.at[q], rl1.at[here], in_plane(q)).start())
    recvl1[here] = loss1[...]
    others(here, PLANE, lambda q: put(loss1, recvl1.at[q], sl1.at[q], rl1.at[q], in_plane(q)).wait_recv())
    loss2[...] = jnp.sum(recvl1[...], axis=0)
    others(z, DEPTHS, lambda k: put(loss2, recvl2.at[z], sl2.at[k], rl2.at[z], in_depth(k)).start())
    recvl2[z] = loss2[...]
    others(z, DEPTHS, lambda k: put(loss2, recvl2.at[k], sl2.at[k], rl2.at[k], in_depth(k)).wait_recv())
    loss_out[...] = jnp.sum(recvl2[...], axis=0)[0:1, 0:1] / seq_total

    halo.wait_send()
    rim.wait_send()
    others(here, PLANE, lambda q: put(send1.at[q], recv1.at[q], s1.at[q], r1.at[q], in_plane(q)).wait_send())
    others(z, DEPTHS, lambda k: put(send2.at[k], recv2.at[k], s2.at[k], r2.at[k], in_depth(k)).wait_send())
    others(z, DEPTHS, lambda k: put(send3.at[k], recv3.at[k], s3.at[k], r3.at[k], in_depth(k)).wait_send())
    others(here, PLANE, lambda q: put(send4.at[q], recv4.at[q], s4.at[q], r4.at[q], in_plane(q)).wait_send())
    others(head, PEERS, lambda k: to_peer(k).wait_send())
    for k in range(PEERS):
        to_before(k).wait_send()
    others(here, PLANE, lambda q: put(loss1, recvl1.at[q], sl1.at[q], rl1.at[q], in_plane(q)).wait_send())
    others(z, DEPTHS, lambda k: put(loss2, recvl2.at[k], sl2.at[k], rl2.at[k], in_depth(k)).wait_send())


def scratch():
    v = pltpu.VMEM
    dma = pltpu.SemaphoreType.DMA
    return [
        v((HALO + ROWS, DEPTH), BF16),
        v((TILES, DEPTH, WIDE), BF16),
        v((TILES, DEPTH, WIDE), BF16),
        v((DEPTH, WIDE), BF16),
        v((HEADS, DEPTH), BF16),
        v((LANES, DEPTH), BF16),
        v((KCONV, HEADS * LANES), F32),
        v((KCONV, WIDE), F32),
        v((1, HEADS * LANES), F32),
        v((1, HEADS * LANES), F32),
        v((1, ROWS), F32),
        v((1, ROWS), jnp.int32),
        v((1, ROWS), jnp.int32),
        v((HALO + ROWS, WIDE), F32),
        v((HEADS, ROWS, LANES), BF16),
        v((ROWS, LANES), F32),
        v((LANES, ROWS), F32),
        v((ROWS, ROWS), F32),
        v((HEADS, ROWS), F32),
        v((HEADS, ROWS), F32),
        v((HEADS, ROWS), F32),
        v((HEADS, LANES), F32),
        v((HEADS, ROWS, LANES), F32),
        v((HEADS, ROWS, LANES), F32),
        v((HEADS, ROWS, LANES), BF16),
        v((PLANE, LANES + 16, LANES), BF16),
        v((PLANE, LANES + 16, LANES), BF16),
        v((PLANE, LANES, LANES), F32),
        v((PLANE, 8, LANES), F32),
        v((DEPTHS, 32, LANES), BF16),
        v((DEPTHS, 32, LANES), BF16),
        v((DEPTHS, 16, LANES), BF16),
        v((DEPTHS, 16, LANES), BF16),
        v((PLANE, LANES, LANES), BF16),
        v((PLANE, LANES, LANES), BF16),
        v((8, ROWS), F32),
        v((PEERS, 8, ROWS), F32),
        v((PEERS, 8, LANES), F32),
        v((8, ROWS + LANES), F32),
        v((8, LANES), F32),
        v((16, ROWS), F32),
        v((8, LANES), F32),
        v((PLANE, 8, LANES), F32),
        v((8, LANES), F32),
        v((DEPTHS, 8, LANES), F32),
        dma((10,)),
        dma((2, TILES)),
        dma((4,)),
        dma((PLANE,)),
        dma((PLANE,)),
        dma((DEPTHS,)),
        dma((DEPTHS,)),
        dma((DEPTHS,)),
        dma((DEPTHS,)),
        dma((PLANE,)),
        dma((PLANE,)),
        dma((PEERS,)),
        dma((PEERS,)),
        dma((PEERS,)),
        dma((PEERS,)),
        dma((PLANE,)),
        dma((PLANE,)),
        dma((DEPTHS,)),
        dma((DEPTHS,)),
    ]


def per_device(
    states,
    inner_weight,
    gate_weight,
    state_weight,
    step_weight,
    step_bias,
    decay_rate,
    skip_gain,
    conv_inner,
    conv_state,
    norm_gain,
    value_weight,
    rewards,
    done_flags,
    horizon,
):
    hbm = pl.BlockSpec(memory_space=pl.ANY)
    smem = pl.BlockSpec(memory_space=pltpu.SMEM)
    vmem = pl.BlockSpec(memory_space=pltpu.VMEM)
    seq_total = states.shape[0] * DEPTHS * PLANE
    values, targets, loss = pl.pallas_call(
        functools.partial(kernel, seq_total),
        out_shape=(
            jax.ShapeDtypeStruct((1, ROWS), F32),
            jax.ShapeDtypeStruct((1, ROWS), F32),
            jax.ShapeDtypeStruct((1, 1), F32),
        ),
        in_specs=[hbm] * 5 + [smem] * 3 + [hbm] * 7,
        out_specs=(vmem, vmem, vmem),
        scratch_shapes=scratch(),
        compiler_params=pltpu.CompilerParams(
            collective_id=0, has_side_effects=True, vmem_limit_bytes=56 * 2**20
        ),
    )(
        states,
        inner_weight,
        gate_weight,
        state_weight,
        step_weight.T,
        step_bias,
        decay_rate,
        skip_gain,
        conv_inner,
        conv_state,
        norm_gain.reshape(1, -1),
        value_weight.reshape(1, -1),
        rewards.reshape(1, -1),
        done_flags.reshape(1, -1),
        horizon.reshape(1, -1),
    )
    return values.reshape(-1), targets.reshape(-1), loss.reshape(())


def solution(mesh):
    torus = Mesh(
        mesh.devices.reshape(DEPTHS, 4, 2, mesh.shape["head"]), SEQ + ("head",)
    )
    placed = (
        P(SEQ, None),
        P(None, "head"),
        P(None, "head"),
        P(),
        P(None, "head"),
        P("head"),
        P("head"),
        P("head"),
        P(None, "head"),
        P(),
        P("head"),
        P("head"),
        P(SEQ),
        P(SEQ),
        P(SEQ),
    )
    return jax.shard_map(
        per_device, mesh=torus, in_specs=placed, out_specs=(P(SEQ), P(SEQ), P()), check_vma=False
    )
```

time: 220 us -> 60.6 us (0.28)
  waiting for transfers between devices: 69.5 us -> 0 us
  Pallas kernels: 0 us -> 55.6 us
  blocking collectives: 48.6 us -> 0 us
  matrix products: 33.4 us -> 0 us
  other arithmetic: 24.5 us -> 0 us
  between operations: 17.5 us -> 2.41 us
  local copies, waits for them, and re-layouts: 16.4 us -> 2.48 us
  starting transfers between devices: 9.22 us -> 0 us
    all_gather x3 -> x0, waiting for transfers between devices: 67.2 us -> none  [entering(): pieces = jax.tree.map(lambda part: lax.all_gather(part, axis), running)]
    pallas_call x0 -> x1, Pallas kernels: none -> 55.6 us  [per_device(): pl.pallas_call(functools.partial(kernel, seq_total), out_shape=(jax.Shape...]
    dot_general x13 -> x0, matrix products: 33.4 us -> none  [the longest x2 7.38 us: block_scan(): block_out = jnp.einsum('tsh,shp->thp', weights, inputs, precision=precise)]
    all_gather x3 -> x0, blocking collectives: 22.6 us -> none  [entering(): pieces = jax.tree.map(lambda part: lax.all_gather(part, axis), running)]
    all_to_all x1 -> x0, blocking collectives: 17.5 us -> none  [from_everyone(): return lax.all_to_all(copies, axis, split_axis=0, concat_axis=0, tiled=True)]
    convert_element_type x9 -> x0, other arithmetic: 9.53 us -> none  [the longest x2 6.52 us: causal_conv(): return jax.nn.silu(summed).astype(jnp.bfloat16)]
    ppermute x2 -> x0, starting transfers between devices: 9.1 us -> none  [from_behind(): return lax.ppermute(block, axis, route)]
    psum x1 -> x0, blocking collectives: 8.47 us -> none  [per_device(): square_sum, value_sum = lax.psum((square_part, value_part), 'head')]
  transfers between devices with their start and end apart: 5 -> 0, of which waited for: 4 -> 0; matrix products, arithmetic and copies ran while one was open for 11% -> 0% of each run, Pallas kernels for 0% -> 0%
where the time goes in v1:
time: 60.6 us; the launch traced here: 60.5 us
  Pallas kernels  55.6 us (92%)
  local copies, waits for them, and re-layouts  2.48 us (4%)
  between operations  2.41 us (4%)
    pallas_call x1, Pallas kernels, per_device(): pl.pallas_call(functools.partial(kernel, seq_total), out_shape=(jax.Shape...  55.6 us
    unnamed x2, local copies, waits for them, and re-layouts  2.48 us

profile of v1, /device:TPU:1, one launch (start us, length us, event | category | flops | bytes accessed | tf_op | source)
XLA Modules:
  0.0 60.5 jit_solution(15680314043078736449)
XLA Ops:
  0.6 55.6 %shard_map.166 = (f32[1,512]{1,0:T(1,128)}, f32[1,512]{1,0:T(1,128)}, f32[1,1]{1,0:T(1,128)}) custom-call(bf16[512,2048]{1,0:T(8,128)(2,1)} %states.1, bf16[2048,1024]{1,0:T(8,128)(2,1)} %w_in.1, bf16[2048,1024]{1,0:T(8,128)(2,1)} %w_gate.1, bf16[2048,256]{1,0:T(8,128)(2,1)} %w_state.1, bf16[8,2048]{1,0:T(8,128)(2,1)} %bitcast.9, f32[8]{0:T(128)} %bias.1, ...), custom_call_target="tpu_custom_call" | custom-call | tf_op jit(solution)/shard_map/pallas_call | solution.py:618
  56.2 1.2 %copy.21 = f32[512]{0:T(512)} copy(f32[512]{0:T(512)} %bitcast.16) | data formatting | bytes 4096
  57.5 1.2 %copy.22 = f32[512]{0:T(512)} copy(f32[512]{0:T(512)} %bitcast.15) | data formatting | bytes 4096

commit v2 on v1

v2 whole, which is shorter than its diff:
```python
import functools

import jax
import jax.numpy as jnp
from jax import lax
from jax.experimental import pallas as pl
from jax.experimental.pallas import tpu as pltpu
from jax.sharding import Mesh
from jax.sharding import PartitionSpec as P

SEQ = ("seq_0", "seq_1", "seq_2")
MESH = pl.DeviceIdType.MESH
F32 = jnp.float32
BF16 = jnp.bfloat16

KCONV = 4
NSTEP = 8
DISCOUNT = 0.99
EXPECTILE = 0.7
EPSILON = 1e-05

HALO = 16
ROWS = 512
HALF = 256
EARLY = 1
DEPTH = 2048
HEADS = 8
LANES = 128
WIDE = 256
TILES = HEADS * LANES // WIDE
PLANE = 8
DEPTHS = 8
PEERS = 4


def silu(value):
    half = 0.5 * value
    return half + half * jnp.tanh(half)


def dot(a, b):
    return jnp.dot(a, b, preferred_element_type=F32)


def three_pieces(value):
    high = value.astype(BF16).astype(F32)
    rest = value - high
    middle = rest.astype(BF16).astype(F32)
    return high, middle, rest - middle


def down(row, rows=LANES):
    return jnp.broadcast_to(row, (rows, row.shape[1])).T


def kernel(
    seq_total,
    states,
    w_in,
    w_gate,
    w_state,
    w_step,
    bias,
    rate,
    skip,
    taps_in,
    taps_st,
    gain,
    weight,
    rewards,
    done,
    horizon,
    out,
    xs,
    wi,
    wg,
    ws,
    wt_in,
    wt,
    tin,
    tst,
    gn,
    vw,
    rw,
    dn,
    hz,
    pre0,
    pre1,
    xh,
    ro,
    rdm,
    wtf,
    sc,
    lrow,
    dtrow,
    drow,
    tail,
    decb,
    recve1,
    dall,
    recve2,
    y,
    gs,
    rs,
    send1,
    recv1,
    inside,
    reach_in,
    send2,
    recv2,
    send4,
    recv4,
    part,
    recvh,
    recvn,
    ext,
    recvr,
    coef,
    loss1,
    recvl,
    local_sem,
    tile_sem,
    near_sem,
    send_sem,
    recv_sem,
    s2,
    r2,
):
    z, x, c, head = (lax.axis_index(name) for name in SEQ + ("head",))
    here = x * 2 + c
    place = z * PLANE + here
    total = DEPTHS * PLANE
    after = lax.rem(place + 1, total)
    before = lax.rem(place + total - 1, total)

    def of_place(at, at_head):
        return (lax.div(at, PLANE), lax.div(lax.rem(at, PLANE), 2), lax.rem(at, 2), at_head)

    def in_plane(q):
        return (z, lax.div(q, 2), lax.rem(q, 2), head)

    def in_depth(k):
        return (k, x, c, head)

    def in_head(k):
        return (z, x, c, k)

    def put(src, dst, ssem, rsem, device):
        return pltpu.make_async_remote_copy(
            src_ref=src, dst_ref=dst, send_sem=ssem, recv_sem=rsem, device_id=device, device_id_type=MESH
        )

    def others(me, count, act):
        def one(i, carry):
            act(lax.rem(me + i, count))
            return carry

        lax.fori_loop(1, count, one, 0)

    def all_of(ref, count, which):
        whole = ref.at[pl.ds(0, count)]
        return put(whole, whole, send_sem.at[which], recv_sem.at[which], in_head(lax.rem(head + 1, PEERS)))

    small = [
        (states, xs.at[pl.ds(HALO, ROWS), :]),
        (w_step, wt_in),
        (done, dn),
        (rewards, rw),
        (w_state, ws),
        (taps_st, tst),
        (taps_in, tin),
        (gain, gn),
        (weight, vw),
        (horizon, hz),
    ]
    local = [pltpu.make_async_copy(src, dst, local_sem.at[i]) for i, (src, dst) in enumerate(small)]

    def tile_copy(src, dst, slot, which):
        columns = pl.ds(pl.multiple_of(which * WIDE, WIDE), WIDE)
        return pltpu.make_async_copy(src.at[:, columns], dst.at[which], tile_sem.at[slot, which])

    def turned(j):
        return lax.rem(j + x, TILES)

    for copy in local:
        copy.start()
    for j in range(TILES):
        tile_copy(w_in, wi, 0, turned(j)).start()
    for j in range(TILES):
        tile_copy(w_gate, wg, 1, j).start()

    barrier = pltpu.get_barrier_semaphore()

    def greet(device):
        pl.semaphore_signal(barrier, inc=1, device_id=device, device_id_type=MESH)

    others(z, DEPTHS, lambda k: greet(in_depth(k)))
    greet(of_place(before, head))
    for k in range(PEERS):
        greet(of_place(after, k))
    others(here, PLANE, lambda q: greet(in_plane(q)))
    others(head, PEERS, lambda k: greet(in_head(k)))

    local[2].wait()
    local[3].wait()
    alive = 1.0 - dn[...].astype(F32)
    ext[...] = jnp.zeros((8, ROWS + LANES), F32)
    ext[0:1, 0:ROWS] = rw[...]
    ext[1:2, 0:ROWS] = alive
    part[...] = jnp.zeros((8, ROWS), F32)
    local[1].wait()
    wt[...] = jnp.concatenate(
        [wt_in[...].astype(F32), jnp.zeros((LANES - HEADS, DEPTH), F32)], axis=0
    ).astype(BF16)
    local[0].wait()

    pl.semaphore_wait(barrier, (PLANE - 1) + (DEPTHS - 1) + (PEERS - 1) + 1 + PEERS)

    halo = put(
        states.at[pl.ds(ROWS - HALO, HALO), :],
        xs.at[pl.ds(0, HALO), :],
        near_sem.at[0],
        near_sem.at[1],
        of_place(after, head),
    )
    halo.start()
    rim = put(
        ext.at[:, pl.ds(0, LANES)], recvr, near_sem.at[2], near_sem.at[3], of_place(before, head)
    )
    rim.start()

    step_pre = lax.dot_general(
        xs[HALO : HALO + ROWS, :],
        wt[...],
        (((1,), (1,)), ((), ())),
        preferred_element_type=F32,
    ).T[0:HEADS, :]
    order = lax.broadcasted_iota(jnp.int32, (HEADS, ROWS), 0)
    bias_rows = jnp.zeros((HEADS, ROWS), F32)
    rate_rows = jnp.zeros((HEADS, ROWS), F32)
    for h in range(HEADS):
        bias_rows = jnp.where(order == h, bias[h], bias_rows)
        rate_rows = jnp.where(order == h, rate[h], rate_rows)
    step_pre = step_pre + bias_rows
    step = jnp.maximum(step_pre, 0.0) + jnp.log1p(jnp.exp(-jnp.abs(step_pre)))
    dtrow[...] = step
    done_rows = jnp.broadcast_to(dn[...].astype(F32), (HEADS, ROWS))
    blocks = ROWS // LANES
    pieces = three_pieces(-(rate_rows * step)) + (done_rows,)
    stacked = jnp.concatenate(
        [p[:, b * LANES : (b + 1) * LANES] for p in pieces for b in range(blocks)], axis=0
    ).astype(BF16)
    triangle = (
        lax.broadcasted_iota(jnp.int32, (LANES, LANES), 0)
        <= lax.broadcasted_iota(jnp.int32, (LANES, LANES), 1)
    ).astype(F32).astype(BF16)
    sums = dot(stacked, triangle)
    span = HEADS * blocks
    decays = sums[0:span] + sums[span : 2 * span] + sums[2 * span : 3 * span]
    dones = sums[3 * span : 4 * span]

    def joined(parts):
        found, offset = [], jnp.zeros((HEADS, 1), F32)
        for b in range(blocks):
            block = parts[b * HEADS : (b + 1) * HEADS, :] + offset
            offset = block[:, LANES - 1 : LANES]
            found.append(block)
        return jnp.concatenate(found, axis=1), offset

    running, last = joined(decays)
    done_to, done_all = joined(dones)
    done_before = done_to - done_rows
    lrow[...] = running
    drow[...] = done_before
    tail[...] = jnp.where(done_before == done_all, jnp.exp(last - running) * step, 0.0)
    lost = jnp.broadcast_to(jnp.where(done_all == 0.0, jnp.exp(last), 0.0), (HEADS, LANES))
    decb[...] = lost
    others(
        here,
        PLANE,
        lambda q: put(decb, recve1.at[here], send_sem.at[0], recv_sem.at[0], in_plane(q)).start(),
    )
    recve1[here] = lost

    def convolved(pre, taps):
        whole = pre[HALO : HALO + HALF, :] * taps[KCONV - 1 : KCONV, :]
        for k in range(KCONV - 1):
            lag = KCONV - 1 - k
            whole = whole + pre[HALO - lag : HALO - lag + HALF, :] * taps[k : k + 1, :]
        return silu(whole)

    def project(pre, half, tile):
        rows = xs[half * HALF : half * HALF + HALO + HALF, :]
        pre[...] = dot(rows, ws[...] if tile is None else wi[tile])

    def finish(pre, half, tile):
        rows = slice(half * HALF, (half + 1) * HALF)
        if tile is None:
            conv = convolved(pre, tst[...])
            wtf[:, rows] = conv[:, 0:LANES].T
            ro[rows, :] = conv[:, LANES:WIDE]
            return
        taps = tin[:, pl.ds(pl.multiple_of(tile * WIDE, WIDE), WIDE)]
        conv = convolved(pre, taps).astype(BF16)
        for k in range(2):
            xh[tile * 2 + k, rows, :] = conv[:, k * LANES : (k + 1) * LANES]

    def gained(tile):
        for k in range(2):
            h = tile * 2 + k
            added = dot((wtf[...] * tail[pl.ds(h, 1), :]).astype(BF16), xh[h])
            send1[h] = added.astype(BF16)

    def send_gained(tile):
        for k in range(2):
            h = tile * 2 + k

            @pl.when(h != here)
            def _():
                put(
                    send1.at[h], recv1.at[here], send_sem.at[1], recv_sem.at[1], in_plane(h)
                ).start()

    def gate_tile(j):
        tile_copy(w_gate, wg, 1, j).wait()
        gate = silu(dot(xs[HALO : HALO + ROWS, :], wg[j]))
        for k in range(2):
            gs[j * 2 + k] = gate[:, k * LANES : (k + 1) * LANES]

    pres = (pre0, pre1)
    tiles = [None] + [turned(j) for j in range(TILES)]

    local[4].wait()
    local[5].wait()
    local[6].wait()
    project(pres[0], 1, None)
    for i in range(1, TILES + 1):
        tile_copy(w_in, wi, 0, tiles[i]).wait()
        project(pres[i % 2], 1, tiles[i])
        finish(pres[(i - 1) % 2], 1, tiles[i - 1])
    finish(pres[TILES % 2], 1, tiles[TILES])

    for j in range(EARLY):
        gate_tile(j)

    halo.wait_recv()
    xs[0:HALO, :] = jnp.where(place > 0, xs[0:HALO, :].astype(F32), 0.0).astype(BF16)
    project(pres[0], 0, None)
    for i in range(1, TILES + 1):
        project(pres[i % 2], 0, tiles[i])
        finish(pres[(i - 1) % 2], 0, tiles[i - 1])
        if i > 1:
            gained(tiles[i - 1])
            send_gained(tiles[i - 1])
    finish(pres[TILES % 2], 0, tiles[TILES])
    gained(tiles[TILES])
    send_gained(tiles[TILES])

    all_of(recve1, PLANE - 1, 0).wait_recv()
    plane_lost = recve1[0]
    for q in range(1, PLANE):
        plane_lost = plane_lost * recve1[q]
    dall[...] = plane_lost
    others(
        z,
        DEPTHS,
        lambda k: put(dall, recve2.at[z], send_sem.at[2], recv_sem.at[2], in_depth(k)).start(),
    )
    recve2[z] = plane_lost
    recv1[here] = send1[here]

    for j in range(EARLY, TILES):
        gate_tile(j)

    all_of(recv1, PLANE - 1, 1).wait_recv()

    def plane_step(q, carry):
        state, lasting = carry
        inside[q] = state
        reach_in[q] = jnp.broadcast_to(lasting, (8, LANES))
        lost = recve1[q, pl.ds(here, 1), :]
        return lost * state + recv1[q].astype(F32), lasting * lost

    state, _ = lax.fori_loop(
        0, PLANE, plane_step, (jnp.zeros((LANES, LANES), F32), jnp.ones((1, LANES), F32))
    )
    send2[...] = state.astype(BF16)

    def to_later(k):
        return put(send2, recv2.at[z], s2.at[k], r2.at[z], in_depth(k))

    def later(act):
        def one(k, carry):
            act(k)
            return carry

        lax.fori_loop(z + 1, DEPTHS, one, 0)

    later(lambda k: to_later(k).start())

    done_row = drow[0:1, :]
    done_down = down(done_row)
    rdm[...] = jnp.where(done_down == 0.0, ro[...], 0.0)
    readout = ro[...].astype(BF16)
    writes_t = wtf[...].astype(BF16)
    for b in range(2):
        rows = slice(b * WIDE, (b + 1) * WIDE)
        upto = (b + 1) * WIDE
        scores = dot(readout[rows, :], writes_t[:, 0:upto])
        at_row = lax.broadcasted_iota(jnp.int32, (WIDE, LANES), 0) + b * WIDE
        for k in range(upto // LANES):
            columns = slice(k * LANES, (k + 1) * LANES)
            at_column = lax.broadcasted_iota(jnp.int32, (WIDE, LANES), 1) + k * LANES
            seen = (at_row >= at_column) & (done_down[rows, :] == done_row[:, columns])
            sc[rows, columns] = jnp.where(seen, scores[:, columns], 0.0)

    def own_scan(h, carry):
        across = lrow[pl.ds(h, 1), :]
        step_across = dtrow[pl.ds(h, 1), :]
        along = down(across)
        inner = xh[h]
        for b in range(2):
            rows = slice(b * WIDE, (b + 1) * WIDE)
            upto = (b + 1) * WIDE
            weights = []
            for k in range(upto // LANES):
                columns = slice(k * LANES, (k + 1) * LANES)
                gap = jnp.minimum(along[rows, :] - across[:, columns], 0.0)
                weights.append((jnp.exp(gap) * step_across[:, columns] * sc[rows, columns]).astype(BF16))
            mixed = dot(jnp.concatenate(weights, axis=1), inner[0:upto, :])
            y[h, rows, :] = mixed + skip[h] * inner[rows, :].astype(F32)
        rs[h] = (rdm[...] * jnp.exp(along)).astype(BF16)
        return carry

    lax.fori_loop(0, HEADS - 2, own_scan, 0)

    all_of(recve2, DEPTHS - 1, 2).wait_recv()

    def depth_step(k, state):
        put(send2, recv2.at[k], s2.at[k], r2.at[k], in_depth(k)).wait_recv()
        return recve2[k, pl.ds(here, 1), :] * state + recv2[k].astype(F32)

    entering = lax.fori_loop(0, z, depth_step, jnp.zeros((LANES, LANES), F32))

    def carried(q):
        send4[q] = (reach_in[q][0:1, :] * entering + inside[q]).astype(BF16)

    def hand_out(q):
        carried(q)
        put(send4.at[q], recv4.at[here], send_sem.at[3], recv_sem.at[3], in_plane(q)).start()

    others(here, PLANE, hand_out)
    carried(here)
    recv4[here] = send4[here]

    lax.fori_loop(HEADS - 2, HEADS, own_scan, 0)

    local[7].wait()
    local[8].wait()
    local[9].wait()
    rim.wait_recv()
    is_last = place == total - 1
    ext[:, ROWS : ROWS + LANES] = jnp.where(is_last, 0.0, recvr[...])
    length = ROWS + LANES
    survive = jnp.ones((1, ROWS), F32)
    rewarded = jnp.zeros((1, ROWS), F32)
    for k in range(NSTEP + 1):
        ahead = ext[...] if k == 0 else pltpu.roll(ext[...], length - k, 1)
        factor = DISCOUNT**k * survive
        rewarded = rewarded + jnp.where(k < hz[...], factor * ahead[0:1, 0:ROWS], 0.0)
        coef[k : k + 1, :] = jnp.where(k == hz[...], factor, 0.0)
        survive = survive * ahead[1:2, 0:ROWS]
    coef[NSTEP + 1 : NSTEP + 2, :] = rewarded
    gn[...] = gn[...] * vw[...]

    all_of(recv4, PLANE - 1, 3).wait_recv()

    def mix(b, carry):
        rows = pl.ds(pl.multiple_of(b * LANES, LANES), LANES)
        squares = jnp.zeros((LANES, LANES), F32)
        valued = jnp.zeros((LANES, LANES), F32)
        for h in range(HEADS):
            mixed = y[h, rows, :] + dot(rs[h, rows, :], recv4[h])
            gated = mixed * gs[h, rows, :]
            squares = squares + gated * gated
            valued = valued + gated * gn[:, h * LANES : (h + 1) * LANES]
        part[0:1, rows] = jnp.sum(squares.T, axis=0, keepdims=True)
        part[1:2, rows] = jnp.sum(valued.T, axis=0, keepdims=True)
        return carry

    lax.fori_loop(0, ROWS // LANES, mix, 0)

    def to_before(k):
        return put(
            part.at[:, pl.ds(0, LANES)],
            recvn.at[head],
            send_sem.at[5],
            recv_sem.at[5],
            of_place(before, k),
        )

    for k in range(PEERS):
        to_before(k).start()
    others(
        head,
        PEERS,
        lambda k: put(part, recvh.at[head], send_sem.at[4], recv_sem.at[4], in_head(k)).start(),
    )
    recvh[head] = part[...]
    all_of(recvh, PEERS - 1, 4).wait_recv()
    all_of(recvn, PEERS, 5).wait_recv()

    def normed(sums):
        return sums[1:2, :] * lax.rsqrt(sums[0:1, :] / (PEERS * HEADS * LANES) + EPSILON)

    own = normed(recvh[0] + recvh[1] + recvh[2] + recvh[3])
    following = normed(recvn[0] + recvn[1] + recvn[2] + recvn[3])
    following = jnp.where(is_last, 0.0, following)
    valued = jnp.broadcast_to(jnp.concatenate([own, following], axis=1), (8, length))
    targets = coef[NSTEP + 1 : NSTEP + 2, :]
    for k in range(NSTEP + 1):
        ahead = valued if k == 0 else pltpu.roll(valued, length - k, 1)
        targets = targets + coef[k : k + 1, :] * ahead[0:1, 0:ROWS]
    residual = targets - own
    terms = jnp.where(residual < 0, 1.0 - EXPECTILE, EXPECTILE) * residual * residual
    mine = jnp.broadcast_to(jnp.sum(terms, axis=1, keepdims=True), (1, LANES))
    loss1[...] = mine

    def tell(device):
        put(loss1, recvl.at[place], send_sem.at[6], recv_sem.at[6], device).start()

    def tell_plane(k):
        for q in range(PLANE):
            tell((k, q // 2, q % 2, head))

    others(z, DEPTHS, tell_plane)
    others(here, PLANE, lambda q: tell(in_plane(q)))
    recvl[place] = mine
    out[0:1, :] = own
    out[1:2, :] = targets

    halo.wait_send()
    rim.wait_send()
    all_of(recve1, PLANE - 1, 0).wait_send()
    all_of(recv1, PLANE - 1, 1).wait_send()
    all_of(recve2, DEPTHS - 1, 2).wait_send()
    all_of(recv4, PLANE - 1, 3).wait_send()
    all_of(recvh, PEERS - 1, 4).wait_send()
    all_of(recvn, PEERS, 5).wait_send()
    later(lambda k: to_later(k).wait_send())

    all_of(recvl, total - 1, 6).wait_recv()
    summed = jnp.sum(recvl[...], axis=0) / seq_total
    out[2:8, :] = jnp.broadcast_to(summed[:, 0:1], (6, ROWS))
    all_of(recvl, total - 1, 6).wait_send()


def scratch():
    v = pltpu.VMEM
    dma = pltpu.SemaphoreType.DMA
    return [
        v((HALO + ROWS, DEPTH), BF16),
        v((TILES, DEPTH, WIDE), BF16),
        v((TILES, DEPTH, WIDE), BF16),
        v((DEPTH, WIDE), BF16),
        v((HEADS, DEPTH), BF16),
        v((LANES, DEPTH), BF16),
        v((KCONV, HEADS * LANES), F32),
        v((KCONV, WIDE), F32),
        v((1, HEADS * LANES), F32),
        v((1, HEADS * LANES), F32),
        v((1, ROWS), F32),
        v((1, ROWS), jnp.int32),
        v((1, ROWS), jnp.int32),
        v((HALO + HALF, WIDE), F32),
        v((HALO + HALF, WIDE), F32),
        v((HEADS, ROWS, LANES), BF16),
        v((ROWS, LANES), F32),
        v((ROWS, LANES), F32),
        v((LANES, ROWS), F32),
        v((ROWS, ROWS), F32),
        v((HEADS, ROWS), F32),
        v((HEADS, ROWS), F32),
        v((HEADS, ROWS), F32),
        v((HEADS, ROWS), F32),
        v((HEADS, LANES), F32),
        v((PLANE, HEADS, LANES), F32),
        v((HEADS, LANES), F32),
        v((DEPTHS, HEADS, LANES), F32),
        v((HEADS, ROWS, LANES), F32),
        v((HEADS, ROWS, LANES), F32),
        v((HEADS, ROWS, LANES), BF16),
        v((PLANE, LANES, LANES), BF16),
        v((PLANE, LANES, LANES), BF16),
        v((PLANE, LANES, LANES), F32),
        v((PLANE, 8, LANES), F32),
        v((LANES, LANES), BF16),
        v((DEPTHS, LANES, LANES), BF16),
        v((PLANE, LANES, LANES), BF16),
        v((PLANE, LANES, LANES), BF16),
        v((8, ROWS), F32),
        v((PEERS, 8, ROWS), F32),
        v((PEERS, 8, LANES), F32),
        v((8, ROWS + LANES), F32),
        v((8, LANES), F32),
        v((16, ROWS), F32),
        v((1, LANES), F32),
        v((DEPTHS * PLANE, 1, LANES), F32),
        dma((10,)),
        dma((2, TILES)),
        dma((4,)),
        dma((7,)),
        dma((7,)),
        dma((DEPTHS,)),
        dma((DEPTHS,)),
    ]


def per_device(
    states,
    inner_weight,
    gate_weight,
    state_weight,
    step_weight,
    step_bias,
    decay_rate,
    skip_gain,
    conv_inner,
    conv_state,
    norm_gain,
    value_weight,
    rewards,
    done_flags,
    horizon,
):
    hbm = pl.BlockSpec(memory_space=pl.ANY)
    smem = pl.BlockSpec(memory_space=pltpu.SMEM)
    vmem = pl.BlockSpec(memory_space=pltpu.VMEM)
    seq_total = states.shape[0] * DEPTHS * PLANE
    packed = pl.pallas_call(
        functools.partial(kernel, seq_total),
        out_shape=jax.ShapeDtypeStruct((8, ROWS), F32),
        in_specs=[hbm] * 5 + [smem] * 3 + [hbm] * 7,
        out_specs=vmem,
        scratch_shapes=scratch(),
        compiler_params=pltpu.CompilerParams(
            collective_id=0, has_side_effects=True, vmem_limit_bytes=56 * 2**20
        ),
    )(
        states,
        inner_weight,
        gate_weight,
        state_weight,
        step_weight.T,
        step_bias,
        decay_rate,
        skip_gain,
        conv_inner,
        conv_state,
        norm_gain.reshape(1, -1),
        value_weight.reshape(1, -1),
        rewards.reshape(1, -1),
        done_flags.reshape(1, -1),
        horizon.reshape(1, -1),
    )
    return packed[0], packed[1], packed[2, 0]


def solution(mesh):
    torus = Mesh(
        mesh.devices.reshape(DEPTHS, 4, 2, mesh.shape["head"]), SEQ + ("head",)
    )
    placed = (
        P(SEQ, None),
        P(None, "head"),
        P(None, "head"),
        P(),
        P(None, "head"),
        P("head"),
        P("head"),
        P("head"),
        P(None, "head"),
        P(),
        P("head"),
        P("head"),
        P(SEQ),
        P(SEQ),
        P(SEQ),
    )
    return jax.shard_map(
        per_device, mesh=torus, in_specs=placed, out_specs=(P(SEQ), P(SEQ), P()), check_vma=False
    )
```

time: 60.6 us -> 55.6 us (0.917)
  Pallas kernels: 55.6 us -> 52.1 us
  between operations: 2.41 us -> 0.65 us
    pallas_call x1, Pallas kernels: 55.6 us -> 52.1 us  [per_device(): pl.pallas_call(functools.partial(kernel, seq_total), out_shape=jax.ShapeD...]
    slice x0 -> x2, local copies, waits for them, and re-layouts: none -> 2.56 us  [per_device(): return (packed[0], packed[1], packed[2, 0])]
    unnamed x2 -> x0, local copies, waits for them, and re-layouts: 2.48 us -> none
where the time goes in v2:
time: 55.6 us; the launch traced here: 55.3 us
  Pallas kernels  52.1 us (94%)
  local copies, waits for them, and re-layouts  2.56 us (5%)
  between operations  0.65 us (1%)
    pallas_call x1, Pallas kernels, per_device(): pl.pallas_call(functools.partial(kernel, seq_total), out_shape=jax.ShapeD...  52.1 us
    slice x2, local copies, waits for them, and re-layouts, per_device(): return (packed[0], packed[1], packed[2, 0])  2.56 us

profile of v2, /device:TPU:1, one launch (start us, length us, event | category | flops | bytes accessed | tf_op | source)
XLA Modules:
  0.0 55.3 jit_solution(10934836849298467287)
XLA Ops:
  0.6 52.1 %shard_map.166 = f32[8,512]{1,0:T(8,128)} custom-call(bf16[512,2048]{1,0:T(8,128)(2,1)} %states.1, bf16[2048,1024]{1,0:T(8,128)(2,1)} %w_in.1, bf16[2048,1024]{1,0:T(8,128)(2,1)} %w_gate.1, bf16[2048,256]{1,0:T(8,128)(2,1)} %w_state.1, bf16[8,2048]{1,0:T(8,128)(2,1)} %bitcast.9, f32[8]{0:T(128)} %bias.1, f32[8]{0:T(128)} %rate.1, f32[8]{0:T(128)} %skip.1, ...), custom_call_target="tpu_custom_call" | custom-call | tf_op jit(solution)/shard_map/pallas_call | solution.py:640
  52.7 1.4 %fusion = (f32[1,512]{1,0:T(1,128)}, f32[1,512]{1,0:T(1,128)}) fusion(f32[8,512]{1,0:T(8,128)} %shard_map.166), kind=kLoop, calls=%fused_computation | loop fusion | bytes 8192 | tf_op jit(solution)/shard_map/slice | solution.py:666
  54.1 1.2 %slice.11 = f32[1,1]{1,0:T(1,128)} slice(f32[8,512]{1,0:T(8,128)} %shard_map.166), slice={[2:3], [0:1]} | slice | bytes 8 | tf_op jit(solution)/shard_map/slice | solution.py:666

commit v3 on v2

--- a/solution.py
+++ b/solution.py
@@ -22,12 +22,14 @@
 HALO = 16
 ROWS = 512
 HALF = 256
-EARLY = 1
+EARLY = 0
 DEPTH = 2048
 HEADS = 8
 LANES = 128
 WIDE = 256
-TILES = HEADS * LANES // WIDE
+TILE = 512
+TILES = HEADS * LANES // TILE
+TILE_HEADS = TILE // LANES
 PLANE = 8
 DEPTHS = 8
 PEERS = 4
@@ -60,9 +62,9 @@
     w_gate,
     w_state,
     w_step,
-    bias,
-    rate,
-    skip,
+    bias_in,
+    rate_in,
+    skip_in,
     taps_in,
     taps_st,
     gain,
@@ -76,6 +78,9 @@
     wg,
     ws,
     wt_in,
+    bias,
+    rate,
+    skip,
     wt,
     tin,
     tst,
@@ -101,7 +106,6 @@
     recve2,
     y,
     gs,
-    rs,
     send1,
     recv1,
     inside,
@@ -164,6 +168,9 @@
     small = [
         (states, xs.at[pl.ds(HALO, ROWS), :]),
         (w_step, wt_in),
+        (bias_in, bias),
+        (rate_in, rate),
+        (skip_in, skip),
         (done, dn),
         (rewards, rw),
         (w_state, ws),
@@ -176,7 +183,7 @@
     local = [pltpu.make_async_copy(src, dst, local_sem.at[i]) for i, (src, dst) in enumerate(small)]
 
     def tile_copy(src, dst, slot, which):
-        columns = pl.ds(pl.multiple_of(which * WIDE, WIDE), WIDE)
+        columns = pl.ds(pl.multiple_of(which * TILE, TILE), TILE)
         return pltpu.make_async_copy(src.at[:, columns], dst.at[which], tile_sem.at[slot, which])
 
     def turned(j):
@@ -186,8 +193,6 @@
         copy.start()
     for j in range(TILES):
         tile_copy(w_in, wi, 0, turned(j)).start()
-    for j in range(TILES):
-        tile_copy(w_gate, wg, 1, j).start()
 
     barrier = pltpu.get_barrier_semaphore()
 
@@ -201,8 +206,8 @@
     others(here, PLANE, lambda q: greet(in_plane(q)))
     others(head, PEERS, lambda k: greet(in_head(k)))
 
-    local[2].wait()
-    local[3].wait()
+    local[5].wait()
+    local[6].wait()
     alive = 1.0 - dn[...].astype(F32)
     ext[...] = jnp.zeros((8, ROWS + LANES), F32)
     ext[0:1, 0:ROWS] = rw[...]
@@ -235,6 +240,8 @@
         (((1,), (1,)), ((), ())),
         preferred_element_type=F32,
     ).T[0:HEADS, :]
+    for i in (2, 3, 4):
+        local[i].wait()
     order = lax.broadcasted_iota(jnp.int32, (HEADS, ROWS), 0)
     bias_rows = jnp.zeros((HEADS, ROWS), F32)
     rate_rows = jnp.zeros((HEADS, ROWS), F32)
@@ -282,38 +289,41 @@
     )
     recve1[here] = lost
 
-    def convolved(pre, taps):
-        whole = pre[HALO : HALO + HALF, :] * taps[KCONV - 1 : KCONV, :]
+    def convolved(pre, taps, columns):
+        whole = pre[HALO : HALO + HALF, columns] * taps[KCONV - 1 : KCONV, :]
         for k in range(KCONV - 1):
             lag = KCONV - 1 - k
-            whole = whole + pre[HALO - lag : HALO - lag + HALF, :] * taps[k : k + 1, :]
+            whole = whole + pre[HALO - lag : HALO - lag + HALF, columns] * taps[k : k + 1, :]
         return silu(whole)
 
     def project(pre, half, tile):
         rows = xs[half * HALF : half * HALF + HALO + HALF, :]
-        pre[...] = dot(rows, ws[...] if tile is None else wi[tile])
+        if tile is None:
+            pre[:, 0:WIDE] = dot(rows, ws[...])
+        else:
+            pre[...] = dot(rows, wi[tile])
 
     def finish(pre, half, tile):
         rows = slice(half * HALF, (half + 1) * HALF)
         if tile is None:
-            conv = convolved(pre, tst[...])
-            wtf[:, rows] = conv[:, 0:LANES].T
-            ro[rows, :] = conv[:, LANES:WIDE]
+            wtf[:, rows] = convolved(pre, tst[:, 0:LANES], slice(0, LANES)).T
+            ro[rows, :] = convolved(pre, tst[:, LANES:WIDE], slice(LANES, WIDE))
             return
-        taps = tin[:, pl.ds(pl.multiple_of(tile * WIDE, WIDE), WIDE)]
-        conv = convolved(pre, taps).astype(BF16)
-        for k in range(2):
-            xh[tile * 2 + k, rows, :] = conv[:, k * LANES : (k + 1) * LANES]
+        for k in range(TILE_HEADS):
+            h = tile * TILE_HEADS + k
+            taps = tin[:, pl.ds(pl.multiple_of(h * LANES, LANES), LANES)]
+            conv = convolved(pre, taps, slice(k * LANES, (k + 1) * LANES))
+            xh[h, rows, :] = conv.astype(BF16)
 
     def gained(tile):
-        for k in range(2):
-            h = tile * 2 + k
+        for k in range(TILE_HEADS):
+            h = tile * TILE_HEADS + k
             added = dot((wtf[...] * tail[pl.ds(h, 1), :]).astype(BF16), xh[h])
             send1[h] = added.astype(BF16)
 
     def send_gained(tile):
-        for k in range(2):
-            h = tile * 2 + k
+        for k in range(TILE_HEADS):
+            h = tile * TILE_HEADS + k
 
             @pl.when(h != here)
             def _():
@@ -324,20 +334,21 @@
     def gate_tile(j):
         tile_copy(w_gate, wg, 1, j).wait()
         gate = silu(dot(xs[HALO : HALO + ROWS, :], wg[j]))
-        for k in range(2):
-            gs[j * 2 + k] = gate[:, k * LANES : (k + 1) * LANES]
+        for k in range(TILE_HEADS):
+            gs[j * TILE_HEADS + k] = gate[:, k * LANES : (k + 1) * LANES]
 
     pres = (pre0, pre1)
     tiles = [None] + [turned(j) for j in range(TILES)]
 
-    local[4].wait()
-    local[5].wait()
-    local[6].wait()
+    for i in (7, 8, 9):
+        local[i].wait()
     project(pres[0], 1, None)
     for i in range(1, TILES + 1):
         tile_copy(w_in, wi, 0, tiles[i]).wait()
         project(pres[i % 2], 1, tiles[i])
         finish(pres[(i - 1) % 2], 1, tiles[i - 1])
+    for j in range(TILES):
+        tile_copy(w_gate, wg, 1, j).start()
     finish(pres[TILES % 2], 1, tiles[TILES])
 
     for j in range(EARLY):
@@ -400,7 +411,7 @@
 
     done_row = drow[0:1, :]
     done_down = down(done_row)
-    rdm[...] = jnp.where(done_down == 0.0, ro[...], 0.0)
+    rdm[...] = jnp.where(done_down == 0.0, ro[...], 0.0).astype(BF16)
     readout = ro[...].astype(BF16)
     writes_t = wtf[...].astype(BF16)
     for b in range(2):
@@ -428,8 +439,8 @@
                 gap = jnp.minimum(along[rows, :] - across[:, columns], 0.0)
                 weights.append((jnp.exp(gap) * step_across[:, columns] * sc[rows, columns]).astype(BF16))
             mixed = dot(jnp.concatenate(weights, axis=1), inner[0:upto, :])
-            y[h, rows, :] = mixed + skip[h] * inner[rows, :].astype(F32)
-        rs[h] = (rdm[...] * jnp.exp(along)).astype(BF16)
+            y[h, rows, :] = (mixed + skip[h] * inner[rows, :].astype(F32)) * gs[h, rows, :]
+        gs[h] = jnp.exp(along) * gs[h]
         return carry
 
     lax.fori_loop(0, HEADS - 2, own_scan, 0)
@@ -455,9 +466,8 @@
 
     lax.fori_loop(HEADS - 2, HEADS, own_scan, 0)
 
-    local[7].wait()
-    local[8].wait()
-    local[9].wait()
+    for i in (10, 11, 12):
+        local[i].wait()
     rim.wait_recv()
     is_last = place == total - 1
     ext[:, ROWS : ROWS + LANES] = jnp.where(is_last, 0.0, recvr[...])
@@ -475,15 +485,18 @@
 
     all_of(recv4, PLANE - 1, 3).wait_recv()
 
+    carried_in = jnp.concatenate([recv4[h] for h in range(HEADS)], axis=1)
+
     def mix(b, carry):
         rows = pl.ds(pl.multiple_of(b * LANES, LANES), LANES)
+        reached = dot(rdm[rows, :], carried_in)
         squares = jnp.zeros((LANES, LANES), F32)
         valued = jnp.zeros((LANES, LANES), F32)
         for h in range(HEADS):
-            mixed = y[h, rows, :] + dot(rs[h, rows, :], recv4[h])
-            gated = mixed * gs[h, rows, :]
+            columns = slice(h * LANES, (h + 1) * LANES)
+            gated = y[h, rows, :] + reached[:, columns] * gs[h, rows, :]
             squares = squares + gated * gated
-            valued = valued + gated * gn[:, h * LANES : (h + 1) * LANES]
+            valued = valued + gated * gn[:, columns]
         part[0:1, rows] = jnp.sum(squares.T, axis=0, keepdims=True)
         part[1:2, rows] = jnp.sum(valued.T, axis=0, keepdims=True)
         return carry
@@ -555,15 +568,24 @@
     all_of(recvl, total - 1, 6).wait_send()
 
 
+def unpack(packed, values, targets, loss):
+    values[...] = packed[0:1, :]
+    targets[...] = packed[1:2, :]
+    loss[...] = packed[2:3, 0:1]
+
+
 def scratch():
     v = pltpu.VMEM
     dma = pltpu.SemaphoreType.DMA
     return [
         v((HALO + ROWS, DEPTH), BF16),
-        v((TILES, DEPTH, WIDE), BF16),
-        v((TILES, DEPTH, WIDE), BF16),
+        v((TILES, DEPTH, TILE), BF16),
+        v((TILES, DEPTH, TILE), BF16),
         v((DEPTH, WIDE), BF16),
         v((HEADS, DEPTH), BF16),
+        pltpu.SMEM((HEADS,), F32),
+        pltpu.SMEM((HEADS,), F32),
+        pltpu.SMEM((HEADS,), F32),
         v((LANES, DEPTH), BF16),
         v((KCONV, HEADS * LANES), F32),
         v((KCONV, WIDE), F32),
@@ -572,11 +594,11 @@
         v((1, ROWS), F32),
         v((1, ROWS), jnp.int32),
         v((1, ROWS), jnp.int32),
-        v((HALO + HALF, WIDE), F32),
-        v((HALO + HALF, WIDE), F32),
+        v((HALO + HALF, TILE), F32),
+        v((HALO + HALF, TILE), F32),
         v((HEADS, ROWS, LANES), BF16),
         v((ROWS, LANES), F32),
-        v((ROWS, LANES), F32),
+        v((ROWS, LANES), BF16),
         v((LANES, ROWS), F32),
         v((ROWS, ROWS), F32),
         v((HEADS, ROWS), F32),
@@ -589,7 +611,6 @@
         v((DEPTHS, HEADS, LANES), F32),
         v((HEADS, ROWS, LANES), F32),
         v((HEADS, ROWS, LANES), F32),
-        v((HEADS, ROWS, LANES), BF16),
         v((PLANE, LANES, LANES), BF16),
         v((PLANE, LANES, LANES), BF16),
         v((PLANE, LANES, LANES), F32),
@@ -606,7 +627,7 @@
         v((16, ROWS), F32),
         v((1, LANES), F32),
         v((DEPTHS * PLANE, 1, LANES), F32),
-        dma((10,)),
+        dma((13,)),
         dma((2, TILES)),
         dma((4,)),
         dma((7,)),
@@ -634,13 +655,12 @@
     horizon,
 ):
     hbm = pl.BlockSpec(memory_space=pl.ANY)
-    smem = pl.BlockSpec(memory_space=pltpu.SMEM)
     vmem = pl.BlockSpec(memory_space=pltpu.VMEM)
     seq_total = states.shape[0] * DEPTHS * PLANE
     packed = pl.pallas_call(
         functools.partial(kernel, seq_total),
         out_shape=jax.ShapeDtypeStruct((8, ROWS), F32),
-        in_specs=[hbm] * 5 + [smem] * 3 + [hbm] * 7,
+        in_specs=[hbm] * 15,
         out_specs=vmem,
         scratch_shapes=scratch(),
         compiler_params=pltpu.CompilerParams(
@@ -663,7 +683,17 @@
         done_flags.reshape(1, -1),
         horizon.reshape(1, -1),
     )
-    return packed[0], packed[1], packed[2, 0]
+    values, targets, loss = pl.pallas_call(
+        unpack,
+        out_shape=(
+            jax.ShapeDtypeStruct((1, ROWS), F32),
+            jax.ShapeDtypeStruct((1, ROWS), F32),
+            jax.ShapeDtypeStruct((1, 1), F32),
+        ),
+        in_specs=[vmem],
+        out_specs=(vmem, vmem, vmem),
+    )(packed)
+    return values.reshape(-1), targets.reshape(-1), loss.reshape(())
 
 
 def solution(mesh):

time: 55.6 us -> 50.3 us (0.905)
  Pallas kernels: 52.1 us -> 49.4 us
  local copies, waits for them, and re-layouts: 2.56 us -> 0 us
    pallas_call x1, Pallas kernels: 52.1 us -> 48.1 us  [per_device(): pl.pallas_call(functools.partial(kernel, seq_total), out_shape=jax.ShapeD...]
    slice x2 -> x0, local copies, waits for them, and re-layouts: 2.56 us -> none  [per_device(): return (packed[0], packed[1], packed[2, 0])]
    pallas_call x0 -> x1, Pallas kernels: none -> 1.3 us  [per_device(): pl.pallas_call(unpack, out_shape=(jax.ShapeDtypeStruct((1, ROWS), F32), j...]
where the time goes in v3:
time: 50.3 us; the launch traced here: 50.1 us
  Pallas kernels  49.4 us (98%)
  between operations  0.64 us (1%)
    pallas_call x1, Pallas kernels, per_device(): pl.pallas_call(functools.partial(kernel, seq_total), out_shape=jax.ShapeD...  48.1 us
    pallas_call x1, Pallas kernels, per_device(): pl.pallas_call(unpack, out_shape=(jax.ShapeDtypeStruct((1, ROWS), F32), j...  1.3 us

profile of v3, /device:TPU:1, one launch (start us, length us, event | category | flops | bytes accessed | tf_op | source)
XLA Modules:
  0.0 50.1 jit_solution(4158732639991248623)
XLA Ops:
  0.6 48.1 %shard_map.166.packed = f32[8,512]{1,0:T(8,128)} custom-call(bf16[512,2048]{1,0:T(8,128)(2,1)} %states.1, bf16[2048,1024]{1,0:T(8,128)(2,1)} %w_in.1, bf16[2048,1024]{1,0:T(8,128)(2,1)} %w_gate.1, bf16[2048,256]{1,0:T(8,128)(2,1)} %w_state.1, bf16[8,2048]{1,0:T(8,128)(2,1)} %bitcast.9, f32[8]{0:T(128)} %bias_in.1, f32[8]{0:T(128)} %rate_in.1, f32[8]{0:T(128)} %skip_in.1, ...), custom_call_target="tpu_custom_call" | custom-call | tf_op jit(solution)/shard_map/pallas_call | solution.py:660
  48.8 1.3 %shard_map.167 = (f32[1,512]{1,0:T(1,128)}, f32[1,512]{1,0:T(1,128)}, f32[1,1]{1,0:T(1,128)}) custom-call(f32[8,512]{1,0:T(8,128)} %shard_map.166.packed), custom_call_target="tpu_custom_call" | custom-call | tf_op jit(solution)/shard_map/pallas_call | solution.py:686

commit v4 on v3

--- a/solution.py
+++ b/solution.py
@@ -21,8 +21,8 @@
 
 HALO = 16
 ROWS = 512
-HALF = 256
-EARLY = 0
+SPANS = ((0, 128), (128, 384))
+LONGEST = 384
 DEPTH = 2048
 HEADS = 8
 LANES = 128
@@ -72,7 +72,9 @@
     rewards,
     done,
     horizon,
-    out,
+    values_out,
+    targets_out,
+    loss_out,
     xs,
     wi,
     wg,
@@ -114,6 +116,10 @@
     recv2,
     send4,
     recv4,
+    squares,
+    valued_sum,
+    held_values,
+    held_targets,
     part,
     recvh,
     recvn,
@@ -129,6 +135,8 @@
     recv_sem,
     s2,
     r2,
+    r4,
+    out_sem,
 ):
     z, x, c, head = (lax.axis_index(name) for name in SEQ + ("head",))
     here = x * 2 + c
@@ -289,30 +297,32 @@
     )
     recve1[here] = lost
 
-    def convolved(pre, taps, columns):
-        whole = pre[HALO : HALO + HALF, columns] * taps[KCONV - 1 : KCONV, :]
+    def convolved(pre, count, taps, columns):
+        whole = pre[HALO : HALO + count, columns] * taps[KCONV - 1 : KCONV, :]
         for k in range(KCONV - 1):
             lag = KCONV - 1 - k
-            whole = whole + pre[HALO - lag : HALO - lag + HALF, columns] * taps[k : k + 1, :]
+            whole = whole + pre[HALO - lag : HALO - lag + count, columns] * taps[k : k + 1, :]
         return silu(whole)
 
-    def project(pre, half, tile):
-        rows = xs[half * HALF : half * HALF + HALO + HALF, :]
+    def project(pre, part_of, tile):
+        first, count = SPANS[part_of]
+        rows = xs[first : first + HALO + count, :]
         if tile is None:
-            pre[:, 0:WIDE] = dot(rows, ws[...])
+            pre[0 : HALO + count, 0:WIDE] = dot(rows, ws[...])
         else:
-            pre[...] = dot(rows, wi[tile])
-
-    def finish(pre, half, tile):
-        rows = slice(half * HALF, (half + 1) * HALF)
+            pre[0 : HALO + count, :] = dot(rows, wi[tile])
+
+    def finish(pre, part_of, tile):
+        first, count = SPANS[part_of]
+        rows = slice(first, first + count)
         if tile is None:
-            wtf[:, rows] = convolved(pre, tst[:, 0:LANES], slice(0, LANES)).T
-            ro[rows, :] = convolved(pre, tst[:, LANES:WIDE], slice(LANES, WIDE))
+            wtf[:, rows] = convolved(pre, count, tst[:, 0:LANES], slice(0, LANES)).T
+            ro[rows, :] = convolved(pre, count, tst[:, LANES:WIDE], slice(LANES, WIDE))
             return
         for k in range(TILE_HEADS):
             h = tile * TILE_HEADS + k
             taps = tin[:, pl.ds(pl.multiple_of(h * LANES, LANES), LANES)]
-            conv = convolved(pre, taps, slice(k * LANES, (k + 1) * LANES))
+            conv = convolved(pre, count, taps, slice(k * LANES, (k + 1) * LANES))
             xh[h, rows, :] = conv.astype(BF16)
 
     def gained(tile):
@@ -350,9 +360,6 @@
     for j in range(TILES):
         tile_copy(w_gate, wg, 1, j).start()
     finish(pres[TILES % 2], 1, tiles[TILES])
-
-    for j in range(EARLY):
-        gate_tile(j)
 
     halo.wait_recv()
     xs[0:HALO, :] = jnp.where(place > 0, xs[0:HALO, :].astype(F32), 0.0).astype(BF16)
@@ -380,7 +387,7 @@
     recve2[z] = plane_lost
     recv1[here] = send1[here]
 
-    for j in range(EARLY, TILES):
+    for j in range(TILES):
         gate_tile(j)
 
     all_of(recv1, PLANE - 1, 1).wait_recv()
@@ -458,7 +465,7 @@
 
     def hand_out(q):
         carried(q)
-        put(send4.at[q], recv4.at[here], send_sem.at[3], recv_sem.at[3], in_plane(q)).start()
+        put(send4.at[q], recv4.at[here], send_sem.at[3], r4.at[here], in_plane(q)).start()
 
     others(here, PLANE, hand_out)
     carried(here)
@@ -483,25 +490,24 @@
     coef[NSTEP + 1 : NSTEP + 2, :] = rewarded
     gn[...] = gn[...] * vw[...]
 
-    all_of(recv4, PLANE - 1, 3).wait_recv()
-
-    carried_in = jnp.concatenate([recv4[h] for h in range(HEADS)], axis=1)
-
-    def mix(b, carry):
-        rows = pl.ds(pl.multiple_of(b * LANES, LANES), LANES)
-        reached = dot(rdm[rows, :], carried_in)
-        squares = jnp.zeros((LANES, LANES), F32)
-        valued = jnp.zeros((LANES, LANES), F32)
-        for h in range(HEADS):
-            columns = slice(h * LANES, (h + 1) * LANES)
-            gated = y[h, rows, :] + reached[:, columns] * gs[h, rows, :]
-            squares = squares + gated * gated
-            valued = valued + gated * gn[:, columns]
-        part[0:1, rows] = jnp.sum(squares.T, axis=0, keepdims=True)
-        part[1:2, rows] = jnp.sum(valued.T, axis=0, keepdims=True)
+    def mix(h):
+        gated = y[h] + dot(rdm[...], recv4[h]) * gs[h]
+        scale = gn[:, pl.ds(pl.multiple_of(h * LANES, LANES), LANES)]
+        return gated * gated, gated * scale
+
+    squares[...], valued_sum[...] = mix(here)
+
+    def mix_arrived(i, carry):
+        h = lax.rem(here + PLANE - i, PLANE)
+        put(send4.at[h], recv4.at[h], send_sem.at[3], r4.at[h], in_plane(h)).wait_recv()
+        more_squares, more_valued = mix(h)
+        squares[...] = squares[...] + more_squares
+        valued_sum[...] = valued_sum[...] + more_valued
         return carry
 
-    lax.fori_loop(0, ROWS // LANES, mix, 0)
+    lax.fori_loop(1, PLANE, mix_arrived, 0)
+    part[0:1, :] = jnp.sum(squares[...].T, axis=0, keepdims=True)
+    part[1:2, :] = jnp.sum(valued_sum[...].T, axis=0, keepdims=True)
 
     def to_before(k):
         return put(
@@ -549,8 +555,14 @@
     others(z, DEPTHS, tell_plane)
     others(here, PLANE, lambda q: tell(in_plane(q)))
     recvl[place] = mine
-    out[0:1, :] = own
-    out[1:2, :] = targets
+    held_values[...] = own
+    held_targets[...] = targets
+    written = [
+        pltpu.make_async_copy(held_values, values_out, out_sem.at[0]),
+        pltpu.make_async_copy(held_targets, targets_out, out_sem.at[1]),
+    ]
+    for copy in written:
+        copy.start()
 
     halo.wait_send()
     rim.wait_send()
@@ -563,15 +575,19 @@
     later(lambda k: to_later(k).wait_send())
 
     all_of(recvl, total - 1, 6).wait_recv()
-    summed = jnp.sum(recvl[...], axis=0) / seq_total
-    out[2:8, :] = jnp.broadcast_to(summed[:, 0:1], (6, ROWS))
+    loss_out[...] = (jnp.sum(recvl[...], axis=0) / seq_total)[:, 0:1]
+    for copy in written:
+        copy.wait()
     all_of(recvl, total - 1, 6).wait_send()
 
 
-def unpack(packed, values, targets, loss):
-    values[...] = packed[0:1, :]
-    targets[...] = packed[1:2, :]
-    loss[...] = packed[2:3, 0:1]
+def hand_over(values, targets, loss, values_out, targets_out, loss_out, sem):
+    pairs = ((values, values_out), (targets, targets_out), (loss, loss_out))
+    copies = [pltpu.make_async_copy(src, dst, sem.at[i]) for i, (src, dst) in enumerate(pairs)]
+    for copy in copies:
+        copy.start()
+    for copy in copies:
+        copy.wait()
 
 
 def scratch():
@@ -594,8 +610,8 @@
         v((1, ROWS), F32),
         v((1, ROWS), jnp.int32),
         v((1, ROWS), jnp.int32),
-        v((HALO + HALF, TILE), F32),
-        v((HALO + HALF, TILE), F32),
+        v((HALO + LONGEST, TILE), F32),
+        v((HALO + LONGEST, TILE), F32),
         v((HEADS, ROWS, LANES), BF16),
         v((ROWS, LANES), F32),
         v((ROWS, LANES), BF16),
@@ -619,6 +635,10 @@
         v((DEPTHS, LANES, LANES), BF16),
         v((PLANE, LANES, LANES), BF16),
         v((PLANE, LANES, LANES), BF16),
+        v((ROWS, LANES), F32),
+        v((ROWS, LANES), F32),
+        v((1, ROWS), F32),
+        v((1, ROWS), F32),
         v((8, ROWS), F32),
         v((PEERS, 8, ROWS), F32),
         v((PEERS, 8, LANES), F32),
@@ -634,6 +654,8 @@
         dma((7,)),
         dma((DEPTHS,)),
         dma((DEPTHS,)),
+        dma((PLANE,)),
+        dma((2,)),
     ]
 
 
@@ -657,11 +679,16 @@
     hbm = pl.BlockSpec(memory_space=pl.ANY)
     vmem = pl.BlockSpec(memory_space=pltpu.VMEM)
     seq_total = states.shape[0] * DEPTHS * PLANE
-    packed = pl.pallas_call(
+    results = (
+        jax.ShapeDtypeStruct((1, ROWS), F32),
+        jax.ShapeDtypeStruct((1, ROWS), F32),
+        jax.ShapeDtypeStruct((1, 1), F32),
+    )
+    found = pl.pallas_call(
         functools.partial(kernel, seq_total),
-        out_shape=jax.ShapeDtypeStruct((8, ROWS), F32),
+        out_shape=results,
         in_specs=[hbm] * 15,
-        out_specs=vmem,
+        out_specs=(hbm, hbm, vmem),
         scratch_shapes=scratch(),
         compiler_params=pltpu.CompilerParams(
             collective_id=0, has_side_effects=True, vmem_limit_bytes=56 * 2**20
@@ -684,15 +711,12 @@
         horizon.reshape(1, -1),
     )
     values, targets, loss = pl.pallas_call(
-        unpack,
-        out_shape=(
-            jax.ShapeDtypeStruct((1, ROWS), F32),
-            jax.ShapeDtypeStruct((1, ROWS), F32),
-            jax.ShapeDtypeStruct((1, 1), F32),
-        ),
-        in_specs=[vmem],
-        out_specs=(vmem, vmem, vmem),
-    )(packed)
+        hand_over,
+        out_shape=results,
+        in_specs=[hbm] * 3,
+        out_specs=(hbm, hbm, hbm),
+        scratch_shapes=[pltpu.SemaphoreType.DMA((3,))],
+    )(*found)
     return values.reshape(-1), targets.reshape(-1), loss.reshape(())
 
 

time: 50.3 us -> 50.6 us (level)
  no operation moved by 1% of the time
where the time goes in v4:
time: 50.6 us; the launch traced here: 50.5 us
  Pallas kernels  49.8 us (98%)
  between operations  0.64 us (1%)
    pallas_call x1, Pallas kernels, per_device(): pl.pallas_call(functools.partial(kernel, seq_total), out_shape=results, i...  48 us
    pallas_call x1, Pallas kernels, per_device(): pl.pallas_call(hand_over, out_shape=results, in_specs=[hbm] * 3, out_spec...  1.86 us

profile of v4, /device:TPU:1, one launch (start us, length us, event | category | flops | bytes accessed | tf_op | source)
XLA Modules:
  0.0 50.5 jit_solution(1976286845593801746)
XLA Ops:
  0.6 48.0 %shard_map.166 = (f32[1,512]{1,0:T(1,128)}, f32[1,512]{1,0:T(1,128)}, f32[1,1]{1,0:T(1,128)}) custom-call(bf16[512,2048]{1,0:T(8,128)(2,1)} %states.1, bf16[2048,1024]{1,0:T(8,128)(2,1)} %w_in.1, bf16[2048,1024]{1,0:T(8,128)(2,1)} %w_gate.1, bf16[2048,256]{1,0:T(8,128)(2,1)} %w_state.1, bf16[8,2048]{1,0:T(8,128)(2,1)} %bitcast.9, f32[8]{0:T(128)} %bias_in.1, ...), custom_call_target="tpu_custom_call" | custom-call | tf_op jit(solution)/shard_map/pallas_call | solution.py:687
  48.6 1.9 %shard_map.167 = (f32[1,512]{1,0:T(1,128)}, f32[1,512]{1,0:T(1,128)}, f32[1,1]{1,0:T(1,128)}) custom-call(f32[1,512]{1,0:T(1,128)} %get-tuple-element.9.values, f32[1,512]{1,0:T(1,128)} %get-tuple-element.10.targets, f32[1,1]{1,0:T(1,128)} %get-tuple-element.11.loss), custom_call_target="tpu_custom_call" | custom-call | tf_op jit(solution)/shard_map/pallas_call | solution.py:713

commit v5 on v4

--- a/solution.py
+++ b/solution.py
@@ -72,9 +72,7 @@
     rewards,
     done,
     horizon,
-    values_out,
-    targets_out,
-    loss_out,
+    out,
     xs,
     wi,
     wg,
@@ -118,8 +116,6 @@
     recv4,
     squares,
     valued_sum,
-    held_values,
-    held_targets,
     part,
     recvh,
     recvn,
@@ -136,7 +132,6 @@
     s2,
     r2,
     r4,
-    out_sem,
 ):
     z, x, c, head = (lax.axis_index(name) for name in SEQ + ("head",))
     here = x * 2 + c
@@ -197,10 +192,8 @@
     def turned(j):
         return lax.rem(j + x, TILES)
 
-    for copy in local:
-        copy.start()
-    for j in range(TILES):
-        tile_copy(w_in, wi, 0, turned(j)).start()
+    for i in (0, 1, 5, 6, 2, 3, 4, 8, 9, 7):
+        local[i].start()
 
     barrier = pltpu.get_barrier_semaphore()
 
@@ -208,11 +201,13 @@
         pl.semaphore_signal(barrier, inc=1, device_id=device, device_id_type=MESH)
 
     others(z, DEPTHS, lambda k: greet(in_depth(k)))
+    tile_copy(w_in, wi, 0, turned(0)).start()
     greet(of_place(before, head))
     for k in range(PEERS):
         greet(of_place(after, k))
     others(here, PLANE, lambda q: greet(in_plane(q)))
     others(head, PEERS, lambda k: greet(in_head(k)))
+    tile_copy(w_in, wi, 0, turned(1)).start()
 
     local[5].wait()
     local[6].wait()
@@ -226,7 +221,6 @@
         [wt_in[...].astype(F32), jnp.zeros((LANES - HEADS, DEPTH), F32)], axis=0
     ).astype(BF16)
     local[0].wait()
-
     pl.semaphore_wait(barrier, (PLANE - 1) + (DEPTHS - 1) + (PEERS - 1) + 1 + PEERS)
 
     halo = put(
@@ -359,6 +353,8 @@
         finish(pres[(i - 1) % 2], 1, tiles[i - 1])
     for j in range(TILES):
         tile_copy(w_gate, wg, 1, j).start()
+    for i in (10, 11, 12):
+        local[i].start()
     finish(pres[TILES % 2], 1, tiles[TILES])
 
     halo.wait_recv()
@@ -506,8 +502,6 @@
         return carry
 
     lax.fori_loop(1, PLANE, mix_arrived, 0)
-    part[0:1, :] = jnp.sum(squares[...].T, axis=0, keepdims=True)
-    part[1:2, :] = jnp.sum(valued_sum[...].T, axis=0, keepdims=True)
 
     def to_before(k):
         return put(
@@ -518,8 +512,12 @@
             of_place(before, k),
         )
 
-    for k in range(PEERS):
-        to_before(k).start()
+    for first, past in ((0, LANES), (LANES, ROWS)):
+        part[0:1, first:past] = jnp.sum(squares[first:past, :].T, axis=0, keepdims=True)
+        part[1:2, first:past] = jnp.sum(valued_sum[first:past, :].T, axis=0, keepdims=True)
+        if first == 0:
+            for k in range(PEERS):
+                to_before(k).start()
     others(
         head,
         PEERS,
@@ -552,17 +550,19 @@
         for q in range(PLANE):
             tell((k, q // 2, q % 2, head))
 
-    others(z, DEPTHS, tell_plane)
+    def tell_planes(first, past):
+        def one(k, carry):
+            tell_plane(k)
+            return carry
+
+        lax.fori_loop(first, past, one, 0)
+
+    tell_planes(0, z)
+    tell_planes(z + 1, DEPTHS)
     others(here, PLANE, lambda q: tell(in_plane(q)))
     recvl[place] = mine
-    held_values[...] = own
-    held_targets[...] = targets
-    written = [
-        pltpu.make_async_copy(held_values, values_out, out_sem.at[0]),
-        pltpu.make_async_copy(held_targets, targets_out, out_sem.at[1]),
-    ]
-    for copy in written:
-        copy.start()
+    out[0:1, :] = own
+    out[1:2, :] = targets
 
     halo.wait_send()
     rim.wait_send()
@@ -575,19 +575,14 @@
     later(lambda k: to_later(k).wait_send())
 
     all_of(recvl, total - 1, 6).wait_recv()
-    loss_out[...] = (jnp.sum(recvl[...], axis=0) / seq_total)[:, 0:1]
-    for copy in written:
-        copy.wait()
+    out[2:3, 0:LANES] = jnp.sum(recvl[...], axis=0) / seq_total
     all_of(recvl, total - 1, 6).wait_send()
 
 
-def hand_over(values, targets, loss, values_out, targets_out, loss_out, sem):
-    pairs = ((values, values_out), (targets, targets_out), (loss, loss_out))
-    copies = [pltpu.make_async_copy(src, dst, sem.at[i]) for i, (src, dst) in enumerate(pairs)]
-    for copy in copies:
-        copy.start()
-    for copy in copies:
-        copy.wait()
+def unpack(packed, values, targets, loss):
+    values[...] = packed[0:1, :]
+    targets[...] = packed[1:2, :]
+    loss[...] = packed[2:3, 0:1]
 
 
 def scratch():
@@ -637,8 +632,6 @@
         v((PLANE, LANES, LANES), BF16),
         v((ROWS, LANES), F32),
         v((ROWS, LANES), F32),
-        v((1, ROWS), F32),
-        v((1, ROWS), F32),
         v((8, ROWS), F32),
         v((PEERS, 8, ROWS), F32),
         v((PEERS, 8, LANES), F32),
@@ -655,7 +648,6 @@
         dma((DEPTHS,)),
         dma((DEPTHS,)),
         dma((PLANE,)),
-        dma((2,)),
     ]
 
 
@@ -684,11 +676,11 @@
         jax.ShapeDtypeStruct((1, ROWS), F32),
         jax.ShapeDtypeStruct((1, 1), F32),
     )
-    found = pl.pallas_call(
+    packed = pl.pallas_call(
         functools.partial(kernel, seq_total),
-        out_shape=results,
+        out_shape=jax.ShapeDtypeStruct((3, ROWS), F32),
         in_specs=[hbm] * 15,
-        out_specs=(hbm, hbm, vmem),
+        out_specs=vmem,
         scratch_shapes=scratch(),
         compiler_params=pltpu.CompilerParams(
             collective_id=0, has_side_effects=True, vmem_limit_bytes=56 * 2**20
@@ -711,12 +703,11 @@
         horizon.reshape(1, -1),
     )
     values, targets, loss = pl.pallas_call(
-        hand_over,
+        unpack,
         out_shape=results,
-        in_specs=[hbm] * 3,
-        out_specs=(hbm, hbm, hbm),
-        scratch_shapes=[pltpu.SemaphoreType.DMA((3,))],
-    )(*found)
+        in_specs=[vmem],
+        out_specs=(vmem, vmem, vmem),
+    )(packed)
     return values.reshape(-1), targets.reshape(-1), loss.reshape(())
 
 

time: 50.6 us -> 50 us (0.988)
  Pallas kernels: 49.8 us -> 49.2 us
    pallas_call x2, Pallas kernels: 49.8 us -> 49.2 us  [the longest x1 47.9 us: per_device(): pl.pallas_call(functools.partial(kernel, seq_total), out_shape=jax.ShapeD...]
where the time goes in v5:
time: 50 us; the launch traced here: 49.8 us
  Pallas kernels  49.2 us (98%)
  between operations  0.64 us (1%)
    pallas_call x1, Pallas kernels, per_device(): pl.pallas_call(functools.partial(kernel, seq_total), out_shape=jax.ShapeD...  47.9 us
    pallas_call x1, Pallas kernels, per_device(): pl.pallas_call(unpack, out_shape=results, in_specs=[vmem], out_specs=(vme...  1.28 us

profile of v5, /device:TPU:1, one launch (start us, length us, event | category | flops | bytes accessed | tf_op | source)
XLA Modules:
  0.0 49.8 jit_solution(3289722621038704778)
XLA Ops:
  0.6 47.9 %shard_map.166.packed = f32[3,512]{1,0:T(4,128)} custom-call(bf16[512,2048]{1,0:T(8,128)(2,1)} %states.1, bf16[2048,1024]{1,0:T(8,128)(2,1)} %w_in.1, bf16[2048,1024]{1,0:T(8,128)(2,1)} %w_gate.1, bf16[2048,256]{1,0:T(8,128)(2,1)} %w_state.1, bf16[8,2048]{1,0:T(8,128)(2,1)} %bitcast.9, f32[8]{0:T(128)} %bias_in.1, f32[8]{0:T(128)} %rate_in.1, f32[8]{0:T(128)} %skip_in.1, ...), custom_call_target="tpu_custom_call" | custom-call | tf_op jit(solution)/shard_map/pallas_call | solution.py:679
  48.5 1.3 %shard_map.167 = (f32[1,512]{1,0:T(1,128)}, f32[1,512]{1,0:T(1,128)}, f32[1,1]{1,0:T(1,128)}) custom-call(f32[3,512]{1,0:T(4,128)} %shard_map.166.packed), custom_call_target="tpu_custom_call" | custom-call | tf_op jit(solution)/shard_map/pallas_call | solution.py:705

commit v6 on v5

--- a/solution.py
+++ b/solution.py
@@ -23,6 +23,7 @@
 ROWS = 512
 SPANS = ((0, 128), (128, 384))
 LONGEST = 384
+SOONER = 3
 DEPTH = 2048
 HEADS = 8
 LANES = 128
@@ -215,7 +216,6 @@
     ext[...] = jnp.zeros((8, ROWS + LANES), F32)
     ext[0:1, 0:ROWS] = rw[...]
     ext[1:2, 0:ROWS] = alive
-    part[...] = jnp.zeros((8, ROWS), F32)
     local[1].wait()
     wt[...] = jnp.concatenate(
         [wt_in[...].astype(F32), jnp.zeros((LANES - HEADS, DEPTH), F32)], axis=0
@@ -446,7 +446,7 @@
         gs[h] = jnp.exp(along) * gs[h]
         return carry
 
-    lax.fori_loop(0, HEADS - 2, own_scan, 0)
+    lax.fori_loop(0, SOONER, own_scan, 0)
 
     all_of(recve2, DEPTHS - 1, 2).wait_recv()
 
@@ -467,7 +467,7 @@
     carried(here)
     recv4[here] = send4[here]
 
-    lax.fori_loop(HEADS - 2, HEADS, own_scan, 0)
+    lax.fori_loop(SOONER, HEADS, own_scan, 0)
 
     for i in (10, 11, 12):
         local[i].wait()
@@ -632,9 +632,9 @@
         v((PLANE, LANES, LANES), BF16),
         v((ROWS, LANES), F32),
         v((ROWS, LANES), F32),
-        v((8, ROWS), F32),
-        v((PEERS, 8, ROWS), F32),
-        v((PEERS, 8, LANES), F32),
+        v((2, ROWS), F32),
+        v((PEERS, 2, ROWS), F32),
+        v((PEERS, 2, LANES), F32),
         v((8, ROWS + LANES), F32),
         v((8, LANES), F32),
         v((16, ROWS), F32),

time: 50 us -> 49.8 us (level)
  no operation moved by 1% of the time
where the time goes in v6:
time: 49.8 us; the launch traced here: 49.7 us
  Pallas kernels  49 us (98%)
  between operations  0.64 us (1%)
    pallas_call x1, Pallas kernels, per_device(): pl.pallas_call(functools.partial(kernel, seq_total), out_shape=jax.ShapeD...  47.7 us
    pallas_call x1, Pallas kernels, per_device(): pl.pallas_call(unpack, out_shape=results, in_specs=[vmem], out_specs=(vme...  1.28 us

profile of v6, /device:TPU:1, one launch (start us, length us, event | category | flops | bytes accessed | tf_op | source)
XLA Modules:
  0.0 49.7 jit_solution(5351152431994509497)
XLA Ops:
  0.6 47.7 %shard_map.166.packed = f32[3,512]{1,0:T(4,128)} custom-call(bf16[512,2048]{1,0:T(8,128)(2,1)} %states.1, bf16[2048,1024]{1,0:T(8,128)(2,1)} %w_in.1, bf16[2048,1024]{1,0:T(8,128)(2,1)} %w_gate.1, bf16[2048,256]{1,0:T(8,128)(2,1)} %w_state.1, bf16[8,2048]{1,0:T(8,128)(2,1)} %bitcast.9, f32[8]{0:T(128)} %bias_in.1, f32[8]{0:T(128)} %rate_in.1, f32[8]{0:T(128)} %skip_in.1, ...), custom_call_target="tpu_custom_call" | custom-call | tf_op jit(solution)/shard_map/pallas_call | solution.py:679
  48.4 1.3 %shard_map.167 = (f32[1,512]{1,0:T(1,128)}, f32[1,512]{1,0:T(1,128)}, f32[1,1]{1,0:T(1,128)}) custom-call(f32[3,512]{1,0:T(4,128)} %shard_map.166.packed), custom_call_target="tpu_custom_call" | custom-call | tf_op jit(solution)/shard_map/pallas_call | solution.py:705

commit v7 on v6

--- a/solution.py
+++ b/solution.py
@@ -221,20 +221,6 @@
         [wt_in[...].astype(F32), jnp.zeros((LANES - HEADS, DEPTH), F32)], axis=0
     ).astype(BF16)
     local[0].wait()
-    pl.semaphore_wait(barrier, (PLANE - 1) + (DEPTHS - 1) + (PEERS - 1) + 1 + PEERS)
-
-    halo = put(
-        states.at[pl.ds(ROWS - HALO, HALO), :],
-        xs.at[pl.ds(0, HALO), :],
-        near_sem.at[0],
-        near_sem.at[1],
-        of_place(after, head),
-    )
-    halo.start()
-    rim = put(
-        ext.at[:, pl.ds(0, LANES)], recvr, near_sem.at[2], near_sem.at[3], of_place(before, head)
-    )
-    rim.start()
 
     step_pre = lax.dot_general(
         xs[HALO : HALO + ROWS, :],
@@ -284,6 +270,22 @@
     tail[...] = jnp.where(done_before == done_all, jnp.exp(last - running) * step, 0.0)
     lost = jnp.broadcast_to(jnp.where(done_all == 0.0, jnp.exp(last), 0.0), (HEADS, LANES))
     decb[...] = lost
+
+    pl.semaphore_wait(barrier, (PLANE - 1) + (DEPTHS - 1) + (PEERS - 1) + 1 + PEERS)
+
+    halo = put(
+        states.at[pl.ds(ROWS - HALO, HALO), :],
+        xs.at[pl.ds(0, HALO), :],
+        near_sem.at[0],
+        near_sem.at[1],
+        of_place(after, head),
+    )
+    halo.start()
+    rim = put(
+        ext.at[:, pl.ds(0, LANES)], recvr, near_sem.at[2], near_sem.at[3], of_place(before, head)
+    )
+    rim.start()
+
     others(
         here,
         PLANE,

time: 49.8 us -> 48.6 us (0.976)
  Pallas kernels: 49 us -> 47.8 us
    pallas_call x1, Pallas kernels: 47.7 us -> 46.5 us  [per_device(): pl.pallas_call(functools.partial(kernel, seq_total), out_shape=jax.ShapeD...]
where the time goes in v7:
time: 48.6 us; the launch traced here: 48.4 us
  Pallas kernels  47.8 us (98%)
  between operations  0.64 us (1%)
    pallas_call x1, Pallas kernels, per_device(): pl.pallas_call(functools.partial(kernel, seq_total), out_shape=jax.ShapeD...  46.5 us
    pallas_call x1, Pallas kernels, per_device(): pl.pallas_call(unpack, out_shape=results, in_specs=[vmem], out_specs=(vme...  1.28 us

profile of v7, /device:TPU:1, one launch (start us, length us, event | category | flops | bytes accessed | tf_op | source)
XLA Modules:
  0.0 48.4 jit_solution(1371281325371536352)
XLA Ops:
  0.6 46.5 %shard_map.166.packed = f32[3,512]{1,0:T(4,128)} custom-call(bf16[512,2048]{1,0:T(8,128)(2,1)} %states.1, bf16[2048,1024]{1,0:T(8,128)(2,1)} %w_in.1, bf16[2048,1024]{1,0:T(8,128)(2,1)} %w_gate.1, bf16[2048,256]{1,0:T(8,128)(2,1)} %w_state.1, bf16[8,2048]{1,0:T(8,128)(2,1)} %bitcast.9, f32[8]{0:T(128)} %bias_in.1, f32[8]{0:T(128)} %rate_in.1, f32[8]{0:T(128)} %skip_in.1, ...), custom_call_target="tpu_custom_call" | custom-call | tf_op jit(solution)/shard_map/pallas_call | solution.py:681
  47.1 1.3 %shard_map.167 = (f32[1,512]{1,0:T(1,128)}, f32[1,512]{1,0:T(1,128)}, f32[1,1]{1,0:T(1,128)}) custom-call(f32[3,512]{1,0:T(4,128)} %shard_map.166.packed), custom_call_target="tpu_custom_call" | custom-call | tf_op jit(solution)/shard_map/pallas_call | solution.py:707
